TPU v7x, 32 devices: a whole 2x2x4 slice. The times are simulated.
32 devices in a mesh: batch: 16 (over z, y, x), hid: 2 (over core).
Axes of the slice: x: 2, y: 2, z: 4, core: 2. Of those that a mesh axis runs over, the one named last changes fastest.
Arguments:
- raw_maps: bfloat16 [64, 24, 24, 512], P(('batch', 'hid')), may hold values from -32 to 32
- partner: int32 [64], P(('batch', 'hid')), may hold values from 0 to 63, as said below
- ratios: float32 [64], P(('batch', 'hid')), may hold values from 0.3 to 0.7
- offsets: int32 [64, 2], P(('batch', 'hid')), may hold values from 0 to 10
- flip_bits: int32 [64], P(('batch', 'hid')), may hold values 0 or 1
- size_class: int32 [64], P(('batch', 'hid')), may hold values 0 or 1
- proj_in: bfloat16 [512, 512], P(('batch', 'hid')), may hold values from -0.25 to 0.25
- kernel_large: bfloat16 [27, 27, 512], P(None, None, ('batch', 'hid')), may hold values from -0.21875 to 0.21875
- kernel_small: bfloat16 [5, 5, 512], P(None, None, ('batch', 'hid')), may hold values from -1.25 to 1.25
- proj_out: bfloat16 [512, 512], P(('batch', 'hid')), may hold values from -0.25 to 0.25
- norm_gain: bfloat16 [5, 512], P(None, ('batch', 'hid')), may hold values from 0.099609375 to 1.8984375
- norm_bias: bfloat16 [5, 512], P(None, ('batch', 'hid')), may hold values from -2 to 2
- ffn_up: bfloat16 [512, 2048], P('batch', 'hid'), may hold values from -0.25 to 0.25
- ffn_down: bfloat16 [2048, 512], P('hid', 'batch'), may hold values from -0.125 to 0.125
- cotangent: bfloat16 [64, 24, 24, 512], P(('batch', 'hid')), may hold values from -6 to 6
Outputs:
- output: bfloat16 [64, 24, 24, 512], P(('batch', 'hid'))
- grad_raw_maps: float32 [64, 24, 24, 512], P(('batch', 'hid'))
- grad_proj_in: float32 [512, 512], P(('batch', 'hid'))
- grad_kernel_large: float32 [27, 27, 512], P(None, None, ('batch', 'hid'))
- grad_kernel_small: float32 [5, 5, 512], P(None, None, ('batch', 'hid'))
- grad_proj_out: float32 [512, 512], P(('batch', 'hid'))
- grad_norm_gain: float32 [5, 512], P(None, ('batch', 'hid'))
- grad_norm_bias: float32 [5, 512], P(None, ('batch', 'hid'))
- grad_ffn_up: float32 [512, 2048], P('batch', 'hid')
- grad_ffn_down: float32 [2048, 512], P('hid', 'batch')
Inputs may be any that keep to these rules, and one draw needn't show every extreme that they name: partner[i] lies among the images from 2 * (i // 2) - 2 to 2 * (i // 2) + 1, taken modulo 64; where i is a multiple of 2 it lies among the first 2 of these.
All inputs are finite; a program needn't handle non-finite values. No bound on the sum of `flip_bits` or of `size_class` on one device may be relied on, other than what follows from the above.
Results may differ from a plain program's by a relative error of at most 0.02.
Values may be sent and summed in bfloat16 or wider, within the bound.
No kernel may reach another device: no remote copies, remote signals or barrier semaphores. Data moves between devices by JAX's collectives and lax.ppermute only.
A program may use at most 192 MiB of HBM per device.

v0:
```python
import jax
import jax.numpy as jnp
from jax import lax
from jax.sharding import PartitionSpec as P

CANVAS = 24
SMALL = 14


EPS = 1e-05


def shifted(block, axis, distance):
    devices = range(lax.axis_size(axis))
    route = [((i - distance) % len(devices), i) for i in devices]
    return lax.ppermute(block, axis, route)


def region(image_sides):
    inside_line = (
        lax.broadcasted_iota(jnp.int32, (image_sides.shape[0], CANVAS), 1) < image_sides[:, None]
    )
    return (inside_line[:, :, None] & inside_line[:, None, :]).astype(jnp.float32)[:, :, :, None]


def place_image(image_map, offset_pair, flip_bit, side_length):
    turned = jnp.where(flip_bit > 0, image_map[:, ::-1, :], image_map)
    padded = jnp.pad(turned, ((0, CANVAS), (0, CANVAS), (0, 0)))
    corner = jnp.minimum(offset_pair, CANVAS - side_length)
    anchor = jnp.zeros((), jnp.int32)
    return lax.dynamic_slice(
        padded, (corner[0], corner[1], anchor), (CANVAS, CANVAS, image_map.shape[2])
    )


def convolve(values, kernel):
    channels = values.shape[3]
    return lax.conv_general_dilated(
        values,
        kernel[:, :, None, :],
        (1, 1),
        "SAME",
        dimension_numbers=("NHWC", "HWIO", "NHWC"),
        feature_group_count=channels,
        preferred_element_type=jnp.float32,
    )


def kernel_grad(spread, gradient, extent):
    channels = spread.shape[3]
    radius = (extent - 1) // 2
    result = lax.conv_general_dilated(
        spread,
        gradient,
        (1, 1),
        ((radius, radius), (radius, radius)),
        dimension_numbers=("CHWN", "IHWO", "NHWC"),
        batch_group_count=channels,
        preferred_element_type=jnp.float32,
    )
    return result[0]


def statistics(stacked, region_mask, gain_rows, bias_rows):
    totals = jnp.sum(stacked * region_mask, axis=(1, 2, 3))
    squares = jnp.sum(stacked * stacked * region_mask, axis=(1, 2, 3))
    pixels = jnp.sum(region_mask)
    totals, squares, pixels = lax.psum((totals, squares, pixels), ("batch", "hid"))
    average = totals / pixels
    inverse = lax.rsqrt(squares / pixels - average * average + EPS)
    normal = (stacked - average[:, None, None, None, :]) * inverse[:, None, None, None, :]
    result = normal * gain_rows[:, None, None, None, :] + bias_rows[:, None, None, None, :]
    return (result, normal, inverse, pixels)


def norm_back(gradient, normal, inverse, gain_rows, pixels, region_mask):
    gradient = gradient * region_mask
    by_bias = jnp.sum(gradient, axis=(1, 2, 3))
    by_gain = jnp.sum(gradient * normal, axis=(1, 2, 3))
    by_bias, by_gain = lax.psum((by_bias, by_gain), ("batch", "hid"))
    factor = (gain_rows * inverse)[:, None, None, None, :]
    centered = (
        gradient
        - (by_bias[:, None, None, None, :] + normal * by_gain[:, None, None, None, :]) / pixels
    )
    return (region_mask * factor * centered, by_gain, by_bias)


def ffn_back(rows_in, hidden_pre, hidden, grad_rows, down_used):
    grad_hidden = jnp.einsum(
        "nhwc,fc->nhwf", grad_rows, down_used, preferred_element_type=jnp.float32
    )
    grad_down = jnp.einsum("nhwf,nhwc->fc", hidden, grad_rows, preferred_element_type=jnp.float32)
    _, gelu_back = jax.vjp(jax.nn.gelu, hidden_pre)
    grad_pre = gelu_back(grad_hidden)[0].astype(jnp.bfloat16)
    grad_up = jnp.einsum("nhwc,nhwf->cf", rows_in, grad_pre, preferred_element_type=jnp.float32)
    return (grad_pre, grad_up, grad_down)


def shards(
    raw_maps,
    partner,
    ratios,
    offsets,
    flip_bits,
    size_class,
    proj_in,
    kernel_large,
    kernel_small,
    proj_out,
    norm_gain,
    norm_bias,
    ffn_up,
    ffn_down,
    cotangent,
):
    images = raw_maps.shape[0]
    position = lax.axis_index(("batch", "hid"))
    everyone = lax.axis_size(("batch", "hid")) * images
    earlier = shifted(raw_maps, ("batch", "hid"), 1)
    candidates = jnp.concatenate([earlier, raw_maps], axis=0)
    relative = jnp.mod(partner - (position * images - images), everyone)
    chooser = (
        relative[:, None] == lax.broadcasted_iota(jnp.int32, (images, 2 * images), 1)
    ).astype(jnp.bfloat16)
    partners = jnp.einsum("ip,phwc->ihwc", chooser, candidates, preferred_element_type=jnp.float32)
    mix_weight = ratios[:, None, None, None]
    mixed_maps = mix_weight * raw_maps.astype(jnp.float32) + (1.0 - mix_weight) * partners
    image_sides = SMALL + (CANVAS - SMALL) * size_class
    region_mask = region(image_sides)
    placed, crop_back = jax.vjp(
        lambda mix_maps: jax.vmap(place_image)(mix_maps, offsets, flip_bits, image_sides),
        mixed_maps,
    )
    inputs = region_mask * placed
    w_in, w_out, k_large, k_small, gain_low, bias_low = (
        lax.all_gather(proj_in, ("batch", "hid"), axis=0, tiled=True),
        lax.all_gather(proj_out, ("batch", "hid"), axis=0, tiled=True),
        lax.all_gather(kernel_large, ("batch", "hid"), axis=2, tiled=True),
        lax.all_gather(kernel_small, ("batch", "hid"), axis=2, tiled=True),
        lax.all_gather(norm_gain, ("batch", "hid"), axis=1, tiled=True),
        lax.all_gather(norm_bias, ("batch", "hid"), axis=1, tiled=True),
    )
    up_half, down_half = (
        lax.all_gather(ffn_up, "batch", axis=0, tiled=True),
        lax.all_gather(ffn_down, "batch", axis=1, tiled=True),
    )
    gain_all = gain_low.astype(jnp.float32)
    bias_all = bias_low.astype(jnp.float32)
    normed_zero, normal_zero, inverse_zero, pixels = statistics(
        inputs[None], region_mask, gain_all[0:1], bias_all[0:1]
    )
    first_low = (region_mask * normed_zero[0]).astype(jnp.bfloat16)
    inner_pre = jnp.einsum("nhwc,cd->nhwd", first_low, w_in, preferred_element_type=jnp.float32)
    normed_one, normal_one, inverse_one, _ = statistics(
        inner_pre[None], region_mask, gain_all[1:2], bias_all[1:2]
    )
    pre_one = normed_one[0]
    spread = (region_mask * jax.nn.gelu(pre_one)).astype(jnp.bfloat16)
    large_out = convolve(spread, k_large)
    small_out = convolve(spread, k_small)
    normed_two, normal_two, inverse_two, _ = statistics(
        jnp.stack([large_out, small_out]), region_mask, gain_all[2:4], bias_all[2:4]
    )
    pre_two = normed_two[0] + normed_two[1]
    merged = (region_mask * jax.nn.gelu(pre_two)).astype(jnp.bfloat16)
    block_sum = inputs + jnp.einsum(
        "nhwc,cd->nhwd", merged, w_out, preferred_element_type=jnp.float32
    )
    normed_four, normal_four, inverse_four, _ = statistics(
        block_sum[None], region_mask, gain_all[4:5], bias_all[4:5]
    )
    normed = (region_mask * normed_four[0]).astype(jnp.bfloat16)
    rows_in = lax.all_gather(normed, "hid", axis=0, tiled=True)
    hidden_pre = jnp.einsum("nhwc,cf->nhwf", rows_in, up_half, preferred_element_type=jnp.float32)
    hidden = jax.nn.gelu(hidden_pre).astype(jnp.bfloat16)
    rows_here = lax.slice_in_dim(hidden, 0, images * lax.axis_size("hid"), axis=0)
    branch = lax.psum_scatter(
        jnp.einsum(
            "nhwf,fc->nhwc", rows_here, down_half, preferred_element_type=jnp.float32
        ).astype(jnp.bfloat16),
        "hid",
        scatter_dimension=0,
        tiled=True,
    ).astype(jnp.float32)
    output = (block_sum + branch).astype(jnp.bfloat16)
    upstream = cotangent.astype(jnp.float32)
    grad_rows = lax.all_gather(cotangent, "hid", axis=0, tiled=True)
    grad_pre, grad_up, grad_down = ffn_back(rows_in, hidden_pre, hidden, grad_rows, down_half)
    rows_here = lax.slice_in_dim(grad_pre, 0, images * lax.axis_size("hid"), axis=0)
    grad_normed = lax.psum_scatter(
        jnp.einsum("nhwf,cf->nhwc", rows_here, up_half, preferred_element_type=jnp.float32).astype(
            jnp.bfloat16
        ),
        "hid",
        scatter_dimension=0,
        tiled=True,
    ).astype(jnp.float32)
    grad_up, grad_down = (
        lax.psum_scatter(grad_up, "batch", scatter_dimension=0, tiled=True),
        lax.psum_scatter(grad_down, "batch", scatter_dimension=1, tiled=True),
    )
    grad_four, gain_four, bias_four = norm_back(
        grad_normed[None], normal_four, inverse_four, gain_all[4:5], pixels, region_mask
    )
    grad_block = upstream + grad_four[0]
    grad_branch = grad_block.astype(jnp.bfloat16)
    grad_out = jnp.einsum("nhwc,nhwd->cd", merged, grad_branch, preferred_element_type=jnp.float32)
    grad_merged = jnp.einsum(
        "nhwd,cd->nhwc", grad_branch, w_out, preferred_element_type=jnp.float32
    )
    _, second_back = jax.vjp(jax.nn.gelu, pre_two)
    grad_pre_two = second_back(region_mask * grad_merged)[0]
    grad_two, gain_two, bias_two = norm_back(
        jnp.stack([grad_pre_two, grad_pre_two]),
        normal_two,
        inverse_two,
        gain_all[2:4],
        pixels,
        region_mask,
    )
    grad_convs = grad_two.astype(jnp.bfloat16)
    grad_large_map = grad_convs[0]
    grad_small_map = grad_convs[1]
    grad_spread = convolve(grad_large_map, k_large[::-1, ::-1, :]) + convolve(
        grad_small_map, k_small[::-1, ::-1, :]
    )
    grad_large = kernel_grad(spread, grad_large_map, k_large.shape[0])
    grad_small = kernel_grad(spread, grad_small_map, k_small.shape[0])
    _, first_back = jax.vjp(jax.nn.gelu, pre_one)
    grad_pre_one = first_back(region_mask * grad_spread)[0]
    grad_one, gain_one, bias_one = norm_back(
        grad_pre_one[None], normal_one, inverse_one, gain_all[1:2], pixels, region_mask
    )
    grad_inner = grad_one[0].astype(jnp.bfloat16)
    grad_in = jnp.einsum("nhwc,nhwd->cd", first_low, grad_inner, preferred_element_type=jnp.float32)
    grad_first = jnp.einsum("nhwd,cd->nhwc", grad_inner, w_in, preferred_element_type=jnp.float32)
    grad_zero, gain_zero, bias_zero = norm_back(
        grad_first[None], normal_zero, inverse_zero, gain_all[0:1], pixels, region_mask
    )
    grad_inputs = grad_block + grad_zero[0]
    grad_in, grad_out, grad_large, grad_small = (
        lax.psum_scatter(grad_in, ("batch", "hid"), scatter_dimension=0, tiled=True),
        lax.psum_scatter(grad_out, ("batch", "hid"), scatter_dimension=0, tiled=True),
        lax.psum_scatter(grad_large, ("batch", "hid"), scatter_dimension=2, tiled=True),
        lax.psum_scatter(grad_small, ("batch", "hid"), scatter_dimension=2, tiled=True),
    )
    grad_mixed = crop_back(region_mask * grad_inputs)[0]
    giving = (1.0 - mix_weight) * grad_mixed
    grad_pool = jnp.einsum(
        "ip,ihwc->phwc", chooser.astype(jnp.float32), giving, precision=lax.Precision.HIGHEST
    )
    returned = shifted(grad_pool[:images].astype(jnp.bfloat16), ("batch", "hid"), -1).astype(
        jnp.float32
    )
    grad_raw = mix_weight * grad_mixed + grad_pool[images:] + returned
    gain_grads = jnp.concatenate([gain_zero, gain_one, gain_two, gain_four], axis=0)
    bias_grads = jnp.concatenate([bias_zero, bias_one, bias_two, bias_four], axis=0)
    share_width = gain_grads.shape[1] // lax.axis_size(("batch", "hid"))
    own_gain = lax.dynamic_slice_in_dim(gain_grads, position * share_width, share_width, 1)
    own_bias = lax.dynamic_slice_in_dim(bias_grads, position * share_width, share_width, 1)
    return (
        output,
        grad_raw,
        grad_in,
        grad_large,
        grad_small,
        grad_out,
        own_gain,
        own_bias,
        grad_up,
        grad_down,
    )


def solution(mesh):
    return jax.shard_map(
        shards,
        mesh=mesh,
        in_specs=(
            P(("batch", "hid"), None, None, None),
            P(("batch", "hid")),
            P(("batch", "hid")),
            P(("batch", "hid"), None),
            P(("batch", "hid")),
            P(("batch", "hid")),
            P(("batch", "hid"), None),
            P(None, None, ("batch", "hid")),
            P(None, None, ("batch", "hid")),
            P(("batch", "hid"), None),
            P(None, ("batch", "hid")),
            P(None, ("batch", "hid")),
            P("batch", "hid"),
            P("hid", "batch"),
            P(("batch", "hid"), None, None, None),
        ),
        out_specs=(
            P(("batch", "hid"), None, None, None),
            P(("batch", "hid"), None, None, None),
            P(("batch", "hid"), None),
            P(None, None, ("batch", "hid")),
            P(None, None, ("batch", "hid")),
            P(("batch", "hid"), None),
            P(None, ("batch", "hid")),
            P(None, ("batch", "hid")),
            P("batch", "hid"),
            P("hid", "batch"),
        ),
        check_vma=False,
    )
```

profile of v0, /device:TPU:0, one launch (start us, length us, event | category | flops | bytes accessed | tf_op | source)
XLA Modules:
  0.0 2260.5 jit_solution(15497575288877879075)
XLA Ops:
  11.4 48.6 %all-gather = bf16[32,16,5]{1,2,0:T(8,128)(2,1)S(1)} all-gather(bf16[1,16,5]{1,2,0:T(8,128)(2,1)S(1)} %bitcast.282), channel_id=1, replica_groups=mesh['batch'=16,'hid'=2] {'batch','hid'}, dimensions={0}, use_global_device_ids=true | all-gather | bytes 5280 | tf_op jit(solution)/shard_map/all_gather | solution.py:141
  63.4 36.9 %all-gather.1 = bf16[32,16,5]{1,2,0:T(8,128)(2,1)S(1)} all-gather(bf16[1,16,5]{1,2,0:T(8,128)(2,1)S(1)} %bitcast.283), channel_id=1, replica_groups=mesh['batch'=16,'hid'=2] {'batch','hid'}, dimensions={0}, use_global_device_ids=true | all-gather | bytes 5280 | tf_op jit(solution)/shard_map/all_gather | solution.py:142
  100.8 40.8 %all_gather.34 = bf16[5,5,512]{1,0,2:T(8,128)(2,1)S(1)} all-gather(bf16[5,5,16]{1,0,2:T(8,128)(2,1)S(1)} %copy.185), channel_id=1, replica_groups=mesh['batch'=16,'hid'=2] {'batch','hid'}, dimensions={2}, use_global_device_ids=true | all-gather | bytes 26400 | tf_op jit(solution)/shard_map/all_gather | solution.py:140
  143.9 50.7 %all_gather.33 = bf16[27,27,512]{1,2,0:T(8,128)(2,1)S(1)} all-gather(bf16[27,27,16]{1,2,0:T(8,128)(2,1)} %param.22), channel_id=1, replica_groups=mesh['batch'=16,'hid'=2] {'batch','hid'}, dimensions={2}, use_global_device_ids=true | all-gather | bytes 769824 | tf_op jit(solution)/shard_map/all_gather | solution.py:139
  194.6 5.3 copy.182
  203.6 40.3 %all_gather.32 = bf16[512,512]{1,0:T(8,128)(2,1)S(1)} all-gather(bf16[16,512]{1,0:T(8,128)(2,1)} %param.21), channel_id=1, replica_groups=mesh['batch'=16,'hid'=2] {'batch','hid'}, dimensions={0}, use_global_device_ids=true | all-gather | bytes 540672 | tf_op jit(solution)/shard_map/all_gather | solution.py:137
  243.8 38.5 %all_gather.35 = bf16[512,512]{1,0:T(8,128)(2,1)S(1)} all-gather(bf16[16,512]{1,0:T(8,128)(2,1)} %param.24), channel_id=1, replica_groups=mesh['batch'=16,'hid'=2] {'batch','hid'}, dimensions={0}, use_global_device_ids=true | all-gather | bytes 540672 | tf_op jit(solution)/shard_map/all_gather | solution.py:138
  282.3 5.5 multiply_add_fusion.3
  290.6 10.2 pad.9
  300.8 11.3 while.2
  301.4 4.8 constant_dynamic-slice_fusion.9
  307.0 4.8 constant_dynamic-slice_fusion.9
  312.6 37.2 %all-reduce.8 = (f32[1,512]{1,0:T(1,128)S(1)}, f32[]{:T(128)}, f32[1,512]{1,0:T(1,128)S(1)}) all-reduce(f32[1,512]{1,0:T(1,128)S(1)} %bitcast.271, f32[]{:T(128)} %convert_reduce_fusion, f32[1,512]{1,0:T(1,128)S(1)} %bitcast.270), channel_id=1, replica_groups=mesh['batch'=16,'hid'=2] {'batch','hid'}, use_global_device_ids=true, to_apply=%region_1.2 | all-reduce | flops 1025 | bytes 8200 | tf_op jit(solution)/shard_map/psum | solution.py:68
  353.8 42.9 %all-reduce.7 = (f32[1,512]{1,0:T(1,128)S(1)}, f32[1,512]{1,0:T(1,128)S(1)}) all-reduce(f32[1,512]{1,0:T(1,128)S(1)} %bitcast.287, f32[1,512]{1,0:T(1,128)S(1)} %bitcast.286), channel_id=1, replica_groups=mesh['batch'=16,'hid'=2] {'batch','hid'}, use_global_device_ids=true, to_apply=%region_7.8 | all-reduce | flops 1024 | bytes 8192 | tf_op jit(solution)/shard_map/psum | solution.py:68
  407.7 6.6 broadcast_select_fusion.2
  418.0 166.8 %fusion.89 = f32[2,24,24,512]{3,0,2,1:T(2,128)S(1)} fusion(bf16[27,27,1,512]{3,2,1,0:T(2,128)(2,1)S(1)} %copy-done.24, bf16[2,24,24,512]{3,2,1,0:T(8,128)(2,1)S(1)} %copy-done.25), kind=kOutput, calls=%fused_computation.142 | convolution fusion | flops 444735488 | bytes 4285440 | tf_op jit(solution)/shard_map/conv_general_dilated | solution.py:38
  586.7 38.4 %all-reduce.6 = (f32[2,512]{1,0:T(2,128)S(1)}, f32[2,512]{1,0:T(2,128)S(1)}) all-reduce(f32[2,512]{1,0:T(2,128)S(1)} %get-tuple-element.97, f32[2,512]{1,0:T(2,128)S(1)} %get-tuple-element.96), channel_id=1, replica_groups=mesh['batch'=16,'hid'=2] {'batch','hid'}, use_global_device_ids=true, to_apply=%region_11.12 | all-reduce | flops 2048 | bytes 16384 | tf_op jit(solution)/shard_map/psum | solution.py:68
  634.7 41.7 %all-reduce.5 = (f32[1,512]{1,0:T(1,128)S(1)}, f32[1,512]{1,0:T(1,128)S(1)}) all-reduce(f32[1,512]{1,0:T(1,128)S(1)} %bitcast.289, f32[1,512]{1,0:T(1,128)S(1)} %bitcast.288), channel_id=1, replica_groups=mesh['batch'=16,'hid'=2] {'batch','hid'}, use_global_device_ids=true, to_apply=%region_15.16 | all-reduce | flops 1024 | bytes 8192 | tf_op jit(solution)/shard_map/psum | solution.py:68
  682.3 8.8 all-gather.7.cloned.1.call-done
  691.0 11.6 multiply_convert_fusion
  702.6 47.6 %all-gather.11.cloned.1.call-done = bf16[1024,512]{0,1:T(8,128)(2,1)} async-done(((bf16[1024,32]{0,1:T(8,128)(2,1)}), bf16[1024,512]{0,1:T(8,128)(2,1)}) %all-gather.11.cloned.1.call-update) | async-done | bytes 1048592 | tf_op jit(solution)/shard_map/all_gather | solution.py:146
  750.3 11.2 all-gather.13.cloned.1.call-done
  761.5 11.0 fusion.6
  780.1 6.3 convolution_convert_fusion.1
  793.5 40.8 %all-reduce.4 = (f32[1,512]{1,0:T(1,128)}, f32[1,512]{1,0:T(1,128)}) all-reduce(f32[1,512]{1,0:T(1,128)} %bitcast.261, f32[1,512]{1,0:T(1,128)} %bitcast.260), channel_id=1, replica_groups=mesh['batch'=16,'hid'=2] {'batch','hid'}, use_global_device_ids=true, to_apply=%region_23.24 | all-reduce | flops 1024 | bytes 8192 | tf_op jit(solution)/shard_map/psum | solution.py:80
  843.9 40.4 %all-reduce.3 = (f32[2,512]{1,0:T(2,128)S(1)}, f32[2,512]{1,0:T(2,128)S(1)}) all-reduce(f32[2,512]{1,0:T(2,128)S(1)} %get-tuple-element.101, f32[2,512]{1,0:T(2,128)S(1)} %get-tuple-element.100), channel_id=1, replica_groups=mesh['batch'=16,'hid'=2] {'batch','hid'}, use_global_device_ids=true, to_apply=%region_27.28 | all-reduce | flops 2048 | bytes 16384 | tf_op jit(solution)/shard_map/psum | solution.py:80
  885.0 5.4 fusion.14
  892.0 22.5 fusion.68
  916.5 699.4 %fusion.77 = f32[1,27,27,512]{3,0,2,1:T(1,128)S(1)} fusion(bf16[2,24,24,512]{3,2,1,0:T(8,128)(2,1)} %get-tuple-element.167, bf16[2,24,24,512]{3,2,1,0:T(8,128)(2,1)S(1)} %copy-done.26), kind=kOutput, calls=%fused_computation.130 | convolution fusion | flops 444735488 | bytes 3852288 | tf_op jit(solution)/shard_map/conv_general_dilated | solution.py:52
  1615.9 8.3 copy.226
  1625.8 6.2 fusion.56
  1636.5 37.0 %rev.13 = bf16[27,27,512]{1,2,0:T(8,128)(2,1)} reverse(bf16[27,27,512]{1,2,0:T(8,128)(2,1)S(1)} %copy-done.6), dimensions={0,1} | reverse | bytes 1492992 | tf_op jit(solution)/shard_map/rev | solution.py:225
  1675.7 6.7 copy.191
  1682.5 7.2 fusion.51
  1689.7 183.1 %fusion.79 = f32[2,24,24,512]{3,0,2,1:T(2,128)} fusion(bf16[27,27,1,512]{3,2,1,0:T(2,128)(2,1)S(1)} %copy.191, bf16[2,24,24,512]{3,2,1,0:T(8,128)(2,1)} %get-tuple-element.167), kind=kOutput, calls=%fused_computation.132 | convolution fusion | flops 444735488 | bytes 4285440 | tf_op jit(solution)/shard_map/conv_general_dilated | solution.py:38
  1876.2 6.3 broadcast_select_fusion.1
  1890.3 40.8 %all-reduce.2 = (f32[1,512]{1,0:T(1,128)S(1)}, f32[1,512]{1,0:T(1,128)S(1)}) all-reduce(f32[1,512]{1,0:T(1,128)S(1)} %bitcast.269, f32[1,512]{1,0:T(1,128)S(1)} %bitcast.268), channel_id=1, replica_groups=mesh['batch'=16,'hid'=2] {'batch','hid'}, use_global_device_ids=true, to_apply=%region_31.32 | all-reduce | flops 1024 | bytes 8192 | tf_op jit(solution)/shard_map/psum | solution.py:80
  1937.0 39.9 %all-reduce.1 = (f32[1,512]{1,0:T(1,128)}, f32[1,512]{1,0:T(1,128)}) all-reduce(f32[1,512]{1,0:T(1,128)S(1)} %bitcast.285, f32[1,512]{1,0:T(1,128)S(1)} %bitcast.284), channel_id=1, replica_groups=mesh['batch'=16,'hid'=2] {'batch','hid'}, use_global_device_ids=true, to_apply=%region_35.36 | all-reduce | flops 1024 | bytes 8192 | tf_op jit(solution)/shard_map/psum | solution.py:80
  1981.3 6.6 add_multiply_fusion
  1988.0 8.2 broadcast_in_dim.23.clone
  1996.2 84.5 %while.3 = (s32[]{:T(128)}, f32[2,48,48,512]{3,0,2,1:T(2,128)}, s32[2,4]{1,0:T(2,128)}, f32[2,24,24,512]{3,2,1,0:T(8,128)S(1)}, s32[]{:T(128)}, /*index=5*/s32[4]{0:T(128)S(1)}, s32[]{:T(128)}) while((s32[]{:T(128)}, f32[2,48,48,512]{3,0,2,1:T(2,128)}, s32[2,4]{1,0:T(2,128)}, f32[2,24,24,512]{3,2,1,0:T(8,128)S(1)}, s32[]{:T(128)}, ...), condition=%wide.while_cond.1, body=%wide.while_body.1.sunk | while | flops 589853 | bytes 10617039 | solution.py:31
  1997.5 4.8 constant_dynamic-slice_fusion.11
  2007.8 30.6 %dynamic-update-slice.8 = f32[2,48,48,512]{3,0,2,1:T(2,128)} dynamic-update-slice(f32[2,48,48,512]{3,0,2,1:T(2,128)} %get-tuple-element.277, f32[1,24,24,512]{3,0,2,1:T(1,128)S(1)} %copy.325, s32[]{:T(128)} %bitcast.202, s32[]{:T(128)} %bitcast.203, s32[]{:T(128)} %bitcast.204, s32[]{:T(128)} %constant.28.clone.1..sunk) | dynamic-update-slice | bytes 2359300 | tf_op jit(solution)/shard_map/transpose(jvp(vmap()))/scatter-add
  2050.1 30.6 %dynamic-update-slice.8 = f32[2,48,48,512]{3,0,2,1:T(2,128)} dynamic-update-slice(f32[2,48,48,512]{3,0,2,1:T(2,128)} %get-tuple-element.277, f32[1,24,24,512]{3,0,2,1:T(1,128)S(1)} %copy.325, s32[]{:T(128)} %bitcast.202, s32[]{:T(128)} %bitcast.203, s32[]{:T(128)} %bitcast.204, s32[]{:T(128)} %constant.28.clone.1..sunk) | dynamic-update-slice | bytes 2359300 | tf_op jit(solution)/shard_map/transpose(jvp(vmap()))/scatter-add
  2089.1 6.8 fusion.47
  2106.3 9.8 collective-permute-done.1
  2116.1 4.9 fusion.41
  2124.7 128.7 %reduce-scatter.19.cloned.1.call-done = f32[16,512]{1,0:T(8,128)} async-done(((f32[512,512]{1,0:T(8,128)}), f32[16,512]{1,0:T(8,128)}) %reduce-scatter.19.cloned.1.call-update) | async-done | bytes 32784 | tf_op jit(solution)/shard_map/reduce_scatter | solution.py:244
  (294 shorter events, 152.8 us)
Async XLA Ops:
  7.2 53.7 %copy-start.71 = (f32[2]{0:T(128)S(1)}, f32[2]{0:T(128)}, u32[]{:S(2)}) copy-start(f32[2]{0:T(128)} %param.17) | copy-start | bytes 28
  7.2 54.2 %copy-start.79 = (s32[2]{0:T(128)S(1)}, s32[2]{0:T(128)}, u32[]{:S(2)}) copy-start(s32[2]{0:T(128)} %param.19) | copy-start | bytes 28
  7.2 54.8 %copy-start.70 = (s32[2,2]{1,0:T(2,128)S(1)}, s32[2,2]{1,0:T(2,128)}, u32[]{:S(2)}) copy-start(s32[2,2]{1,0:T(2,128)} %param.18) | copy-start | bytes 52
  7.2 56.2 %copy-start.66 = (bf16[5,16]{1,0:T(8,128)(2,1)S(1)}, bf16[5,16]{1,0:T(8,128)(2,1)}, u32[]{:S(2)}) copy-start(bf16[5,16]{1,0:T(8,128)(2,1)} %param.26) | copy-start | bytes 484
  7.2 93.4 %copy-start.55 = (bf16[5,5,16]{2,1,0:T(8,128)(2,1)S(1)}, bf16[5,5,16]{2,1,0:T(8,128)(2,1)}, u32[]{:S(2)}) copy-start(bf16[5,5,16]{2,1,0:T(8,128)(2,1)} %param.23) | copy-start | bytes 2404
  7.3 675.0 %all-gather.9.cloned.1.call-start = ((), (), s32[]{:S(2)}) async-start(), calls=%async_computation.9 | async-start | bytes 1114112 | tf_op jit(solution)/shard_map/all_gather | solution.py:145
  10.8 271.5 %collective-permute-start = (bf16[2,24,24,512]{3,0,2,1:T(2,128)(2,1)}, bf16[2,24,24,512]{3,0,2,1:T(2,128)(2,1)}, u32[]{:S(2)}, u32[]{:S(2)}) collective-permute-start(bf16[2,24,24,512]{3,0,2,1:T(2,128)(2,1)} %copy.171), channel_id=1, source_target_pairs={{31,0},{0,1},{1,2},{2,3},{3,4},{4,5},{5,6},{6,7},{7,8},{8,9},{9,10... | collective-permute-start | bytes 3538952 | tf_op jit(solution)/shard_map/ppermute | solution.py:16
  11.3 679.7 %all-gather.7.cloned.1.call-start = ((), (), s32[]{:S(2)}) async-start(), calls=%async_computation.8 | async-start | bytes 3538944 | tf_op jit(solution)/shard_map/all_gather | solution.py:174
  11.4 89.2 %copy-start.67 = (pred[2,24]{1,0:T(4,128)(4,1)}, pred[2,24]{1,0:T(4,128)(4,1)S(1)}, u32[]{:S(2)}) copy-start(pred[2,24]{1,0:T(4,128)(4,1)S(1)} %iota_compare_fusion.4) | copy-start | bytes 148
  194.6 5.3 copy-start.5
  202.7 85.1 %copy-start.73 = (s32[2]{0:T(128)}, s32[2]{0:T(128)S(1)}, u32[]{:S(2)}) copy-start(s32[2]{0:T(128)S(1)} %and_select_fusion) | copy-start | bytes 28
  202.8 148.3 %copy-start.68 = (f32[1,512]{1,0:T(1,128)}, f32[1,512]{1,0:T(1,128)S(1)}, u32[]{:S(2)}) copy-start(f32[1,512]{1,0:T(1,128)S(1)} %get-tuple-element.173) | copy-start | bytes 6148
  202.8 196.3 %copy-start.42 = (f32[1,512]{1,0:T(1,128)}, f32[1,512]{1,0:T(1,128)S(1)}, u32[]{:S(2)}) copy-start(f32[1,512]{1,0:T(1,128)S(1)} %get-tuple-element.172) | copy-start | bytes 6148
  203.6 474.1 %copy-start.18 = (f32[2,24,24]{2,1,0:T(8,128)}, f32[2,24,24]{2,1,0:T(8,128)S(1)}, u32[]{:S(2)}) copy-start(f32[2,24,24]{2,1,0:T(8,128)S(1)} %and_convert_fusion) | copy-start | bytes 13828
  243.8 107.2 %copy-start.32 = (bf16[512,512]{1,0:T(8,128)(2,1)}, bf16[512,512]{1,0:T(8,128)(2,1)S(1)}, u32[]{:S(2)}) copy-start(bf16[512,512]{1,0:T(8,128)(2,1)S(1)} %all_gather.32) | copy-start | bytes 1572868
  282.3 347.5 %copy-start.34 = (bf16[512,512]{1,0:T(8,128)(2,1)}, bf16[512,512]{1,0:T(8,128)(2,1)S(1)}, u32[]{:S(2)}) copy-start(bf16[512,512]{1,0:T(8,128)(2,1)S(1)} %all_gather.35) | copy-start | bytes 1572868
  282.3 5.6 copy-start.63
  290.6 10.2 copy-start.14
  312.1 39.0 %copy-start.15 = (f32[2,24,24,512]{3,2,1,0:T(8,128)}, f32[2,24,24,512]{3,2,1,0:T(8,128)S(1)}, u32[]{:S(2)}) copy-start(f32[2,24,24,512]{3,2,1,0:T(8,128)S(1)} %get-tuple-element.17) | copy-start | bytes 7077892
  312.1 37.8 %copy-start.41 = (f32[512,5]{0,1:T(8,128)S(1)}, f32[512,5]{0,1:T(8,128)}, u32[]{:S(2)}) copy-start(f32[512,5]{0,1:T(8,128)} %reshape.288) | copy-start | bytes 30724
  353.8 47.4 %copy-start.2 = (f32[2,24,24,512]{3,2,1,0:T(8,128)}, f32[2,24,24,512]{3,2,1,0:T(8,128)S(1)}, u32[]{:S(2)}) copy-start(f32[2,24,24,512]{3,2,1,0:T(8,128)S(1)} %get-tuple-element.183) | copy-start | bytes 7077892
  585.3 41.0 %copy-start.53 = (f32[2,512]{1,0:T(2,128)S(1)}, f32[2,512]{1,0:T(2,128)}, u32[]{:S(2)}) copy-start(f32[2,512]{1,0:T(2,128)} %slice.121) | copy-start | bytes 12292
  680.9 69.4 %all-gather.11.cloned.1.call-start = ((), (), s32[]{:S(2)}) async-start(), calls=%async_computation.10 | async-start | bytes 1114112 | tf_op jit(solution)/shard_map/all_gather | solution.py:146
  681.6 79.9 %all-gather.13.cloned.1.call-start = ((), (), s32[]{:S(2)}) async-start(), calls=%async_computation.12 | async-start | bytes 3538944 | tf_op jit(solution)/shard_map/all_gather | solution.py:188
  682.2 108.0 %reduce-scatter.13.cloned.1.call-start = ((), (), s32[]{:S(2)}) async-start(), calls=%async_computation.13 | async-start | bytes 3538944 | tf_op jit(solution)/shard_map/reduce_scatter | solution.py:191
  761.5 13.1 copy-start.76
  778.9 1202.4 %reduce-scatter.11.cloned.1.call-start = ((), (), s32[]{:S(2)}) async-start(), calls=%async_computation.11 | async-start | bytes 3538944 | tf_op jit(solution)/shard_map/reduce_scatter | solution.py:178
  786.5 1316.9 %reduce-scatter.25.cloned.1.call-start = ((), (), s32[]{:S(2)}) async-start(), calls=%async_computation.19 | async-start | bytes 270336
  790.2 44.1 %copy-start.10 = (bf16[2,24,24,512]{3,2,1,0:T(8,128)(2,1)S(1)}, bf16[2,24,24,512]{3,2,1,0:T(8,128)(2,1)}, u32[]{:S(2)}) copy-start(bf16[2,24,24,512]{3,2,1,0:T(8,128)(2,1)} %reduce-scatter.13.cloned.1.call-done) | copy-start | bytes 3538948
  838.0 4.5 copy-start.29
  838.0 4.5 copy-start.1
  842.5 42.5 %copy-start.20 = (f32[2,24,24]{2,1,0:T(8,128)S(1)}, f32[2,24,24]{2,1,0:T(8,128)}, u32[]{:S(2)}) copy-start(f32[2,24,24]{2,1,0:T(8,128)} %copy-done.18) | copy-start | bytes 13828
  842.5 42.5 %copy-start.52 = (f32[2,512]{1,0:T(2,128)S(1)}, f32[2,512]{1,0:T(2,128)}, u32[]{:S(2)}) copy-start(f32[2,512]{1,0:T(2,128)} %get-tuple-element.152) | copy-start | bytes 12292
  916.4 1206.5 %reduce-scatter.17.cloned.1.call-start = ((), (), s32[]{:S(2)}) async-start(), calls=%async_computation.15 | async-start | bytes 8650752 | tf_op jit(solution)/shard_map/reduce_scatter | solution.py:245
  1624.2 500.5 %reduce-scatter.21.cloned.1.call-start = ((), (), s32[]{:S(2)}) async-start(), calls=%async_computation.17 | async-start | bytes 2228224 | tf_op jit(solution)/shard_map/reduce_scatter | solution.py:200
  1632.1 4.5 copy-start.6
  1632.1 492.6 %reduce-scatter.23.cloned.1.call-start = ((), (), s32[]{:S(2)}) async-start(), calls=%async_computation.18 | async-start | bytes 2228224 | tf_op jit(solution)/shard_map/reduce_scatter | solution.py:201
  1689.7 183.2 %copy-start.22 = (bf16[24,2,24,512]{3,2,0,1:T(8,128)(2,1)S(1)}, bf16[24,2,24,512]{3,2,0,1:T(8,128)(2,1)}, u32[]{:S(2)}) copy-start(bf16[24,2,24,512]{3,2,0,1:T(8,128)(2,1)} %get-tuple-element.166) | copy-start | bytes 3538948
  1689.7 435.0 %reduce-scatter.15.cloned.1.call-start = ((), (), s32[]{:S(2)}) async-start(), calls=%async_computation.14 | async-start | bytes 1081344 | tf_op jit(solution)/shard_map/reduce_scatter | solution.py:243
  1886.1 45.0 %copy-start.62 = (f32[1,512]{1,0:T(1,128)S(1)}, f32[1,512]{1,0:T(1,128)}, u32[]{:S(2)}) copy-start(f32[1,512]{1,0:T(1,128)} %get-tuple-element.148) | copy-start | bytes 6148
  1976.8 4.5 copy-start.11
  1976.8 4.5 copy-start.46
  1976.8 4.5 copy-start.47
  1981.2 272.2 %reduce-scatter.19.cloned.1.call-start = ((), (), s32[]{:S(2)}) async-start(), calls=%async_computation.16 | async-start | bytes 1081344 | tf_op jit(solution)/shard_map/reduce_scatter | solution.py:244
  1988.0 8.2 copy-start.7
  1988.0 8.2 copy-start.54
  1996.2 84.5 %copy-start.64 = (pred[2]{0:T(512)(128)(4,1)S(1)}, pred[2]{0:T(512)(128)(4,1)}, u32[]{:S(2)}) copy-start(pred[2]{0:T(512)(128)(4,1)} %broadcast_compare_fusion) | copy-start | bytes 10
  2099.1 17.0 collective-permute-start.1
  (49 other events, 121.6 us)
Sparse Core Ops, SparseCore 0:
  11.4 60.3 all-gather.8
  681.0 9.9 all-gather.6
  693.8 56.4 all-gather.10
  751.7 9.7 all-gather.12
  779.0 11.0 reduce-scatter.12
  792.3 11.0 reduce-scatter.10
  916.6 134.4 reduce-scatter.24
  1624.3 149.7 reduce-scatter.16
  1777.0 76.3 reduce-scatter.20
  1856.2 77.7 reduce-scatter.22
  1981.3 135.8 reduce-scatter.14
  2119.9 133.4 reduce-scatter.18
where the time goes:
time: 2270 us; the launch traced here: 2260 us
  matrix products  1160 us (51%)
  blocking collectives  578 us (25%)
  local copies, waits for them, and re-layouts  213 us (9%)
  waiting for transfers between devices  211 us (9%)
  other arithmetic  77 us (3%)
    conv_general_dilated x2, matrix products, kernel_grad(): lax.conv_general_dilated(spread, gradient, (1, 1), ((radius, radius), (ra...  722 us
    conv_general_dilated x4, matrix products, convolve(): lax.conv_general_dilated(values, kernel[:, :, None, :], (1, 1), 'SAME', d...  363 us
    psum x4, blocking collectives, norm_back(): by_bias, by_gain = lax.psum((by_bias, by_gain), ('batch', 'hid'))  162 us
    psum x4, blocking collectives, statistics(): lax.psum((totals, squares, pixels), ('batch', 'hid'))  160 us
    reduce_scatter x1, waiting for transfers between devices, shards(): lax.psum_scatter(grad_out, ('batch', 'hid'), scatter_dimension=0, tiled=T...  129 us
    scatter-add x10, local copies, waits for them, and re-layouts  75.9 us
    all_gather x1, blocking collectives, shards(): lax.all_gather(kernel_large, ('batch', 'hid'), axis=2, tiled=True)  50.7 us
    all_gather x1, blocking collectives, shards(): lax.all_gather(norm_gain, ('batch', 'hid'), axis=1, tiled=True)  48.6 us
  transfers between devices with their start and end apart: 14, of which 6 were waited for; matrix products, arithmetic and copies ran while one was open for 63% of the time, Pallas kernels for 0%

commit v1 on v0

v1 whole, which is shorter than its diff:
```python
import functools

import jax
import jax.numpy as jnp
import ml_dtypes
import numpy as np
from jax import lax
from jax.experimental import pallas as pl
from jax.experimental.pallas import tpu as pltpu
from jax.sharding import PartitionSpec as P

CANVAS = 24
SMALL = 14
SPOTS = CANVAS * CANVAS
EPS = 1e-05
BOTH = ("batch", "hid")
ROOT = float(np.sqrt(2.0 / np.pi))
CUBE = 0.044715
F32 = jnp.float32
BF16 = jnp.bfloat16
STEPS = 4
VMEM = 56 * 1024 * 1024


def frequencies(extent):
    side = CANVAS + (extent - 1) // 2
    half = [(0, v) for v in range(side // 2 + 1)]
    half += [(u, v) for u in range(1, side // 2 + 1) for v in range(side)]
    if side % 2 == 0:
        raise ValueError("even side")
    return side, np.array(half, np.float64)


def waves(points, extent, columns, scaled):
    side, half = frequencies(extent)
    count = -(-len(half) // 16) * 16
    angle = 2.0 * np.pi / side * (half @ np.array(points, np.float64).T)
    weight = np.where(np.arange(len(half)) == 0, 1.0, 2.0)[:, None] / side**2 if scaled else 1.0
    table = np.zeros((2 * count, columns), np.float64)
    table[: len(half), : len(points)] = np.cos(angle) * weight
    table[count : count + len(half), : len(points)] = np.sin(angle) * weight
    return table.astype(ml_dtypes.bfloat16)


def taps(extent):
    radius = (extent - 1) // 2
    return [(a - radius, b - radius) for a in range(extent) for b in range(extent)]


def padded(count):
    return -(-count // 128) * 128


def dot(a, b):
    return lax.dot_general(a, b, (((1,), (0,)), ((), ())), preferred_element_type=F32)


def dot_t(a, b):
    return lax.dot_general(a, b, (((1,), (1,)), ((), ())), preferred_element_type=F32)


def t_dot(a, b):
    return lax.dot_general(a, b, (((0,), (0,)), ((), ())), preferred_element_type=F32)


def gelu_parts(v):
    square = v * v
    bend = jnp.tanh(ROOT * v * (1.0 + CUBE * square))
    half = 0.5 + 0.5 * bend
    slope = half + (0.5 * ROOT) * v * (1.0 - bend * bend) * (1.0 + (3.0 * CUBE) * square)
    return v * half, slope


def gelu(v):
    return v * (0.5 + 0.5 * jnp.tanh(ROOT * v * (1.0 + CUBE * v * v)))


def center(totals, squares, pixels):
    average = totals / pixels
    return average, lax.rsqrt(squares / pixels - average * average + EPS)


def rows_of(*rows):
    return jnp.concatenate(rows, axis=0)


def down(v):
    return jnp.sum(v, axis=0, keepdims=True)


def tell(ref, rows):
    ref[...] = jnp.broadcast_to(rows[None], ref.shape)


def add_up(acc, step, rows):
    @pl.when(step == 0)
    def _():
        acc[...] = rows

    @pl.when(step > 0)
    def _():
        acc[...] += rows


def mix_kernel(images, rel, ratio, sides, own, first, second, target, x_out, st_out, other, acc):
    i = pl.program_id(0)

    @pl.when(rel[i] < images)
    def _():
        other[...] = first[0]

    @pl.when(rel[i] >= images)
    def _():
        other[...] = second[0]

    pick = (target[0] == lax.broadcasted_iota(jnp.int32, (SPOTS, SPOTS), 1)).astype(BF16)
    x = ratio[i] * dot(pick, own[0]) + (1.0 - ratio[i]) * dot(pick, other[...])
    x_out[0] = x
    pixels = jnp.full((1, x.shape[1]), (sides[i] * sides[i]).astype(F32), F32)
    add_up(acc, i, rows_of(down(x), down(x * x), pixels))

    @pl.when(i == images - 1)
    def _():
        tell(st_out, acc[...])


def inner_kernel(steps, st, gb, mask, x, w_in, first_out, inner_out, norm_out, st_out, coef, acc):
    i = pl.program_id(0)

    @pl.when(i == 0)
    def _():
        sums = jnp.sum(st[...], axis=0)
        pixels = sums[2:3]
        average, inverse = center(sums[0:1], sums[1:2], pixels)
        coef[...] = rows_of(average, inverse, pixels)
        norm_out[...] = coef[...]

    scale = coef[1:2] * gb[0:1]
    shift = gb[5:6] - coef[0:1] * scale
    first = ((x[...] * scale + shift) * mask[...]).astype(BF16)
    first_out[...] = first
    inner = dot(first, w_in[...])
    inner_out[...] = inner
    inner = inner * mask[...]
    add_up(acc, i, rows_of(down(inner), down(inner * inner)))

    @pl.when(i == steps - 1)
    def _():
        tell(st_out, acc[...])


def taps_kernel(kt, waves_large, waves_small, large_out, small_out):
    large = waves_large.shape[1]
    large_out[...] = dot_t(waves_large[...], kt[:, :large])
    small_out[...] = dot_t(waves_small[...], kt[:, large:])


def spread_kernel(
    images, st, norm, gb, mask, inner, fourier, back, tap_large, tap_small,
    large_out, small_out, moved_out, norm_out, st_out,
):
    sums = jnp.sum(st[...], axis=0)
    pixels = norm[2:3]
    average, inverse = center(sums[0:1], sums[1:2], pixels)
    norm_out[...] = rows_of(average, inverse)
    scale = inverse * gb[1:2]
    shift = gb[6:7] - average * scale
    half = fourier.shape[0] // 2
    totals = None
    for n in range(images):
        rows = slice(n * SPOTS, (n + 1) * SPOTS)
        here = mask[rows]
        spread = (gelu(inner[rows] * scale + shift) * here).astype(BF16)
        moved = dot(fourier[...], spread)
        moved_out[n] = moved
        mc, ms = moved[:half], moved[half:]
        outs = []
        for tap in (tap_large, tap_small):
            kc, ks = tap[:half], tap[half:]
            both = jnp.concatenate(
                [(mc * kc + ms * ks).astype(BF16), (ms * kc - mc * ks).astype(BF16)], axis=0
            )
            outs.append(dot(back[...], both))
        large_out[rows] = outs[0]
        small_out[rows] = outs[1]
        large, small = outs[0] * here, outs[1] * here
        part = rows_of(down(large), down(large * large), down(small), down(small * small))
        totals = part if totals is None else totals + part
    tell(st_out, totals)


def merge_kernel(steps, st, norm, gb, mask, large, small, x, w_out, merged_out, block_out, norm_out, st_out, coef, acc):
    i = pl.program_id(0)

    @pl.when(i == 0)
    def _():
        sums = jnp.sum(st[...], axis=0)
        pixels = norm[2:3]
        coef[...] = rows_of(*center(sums[0:1], sums[1:2], pixels), *center(sums[2:3], sums[3:4], pixels))
        norm_out[...] = coef[...]

    by_large = coef[1:2] * gb[2:3]
    by_small = coef[3:4] * gb[3:4]
    shift = gb[7:8] + gb[8:9] - coef[0:1] * by_large - coef[2:3] * by_small
    pre = large[...] * by_large + small[...] * by_small + shift
    merged = (gelu(pre) * mask[...]).astype(BF16)
    merged_out[...] = merged
    block = x[...] + dot(merged, w_out[...])
    block_out[...] = block
    block = block * mask[...]
    add_up(acc, i, rows_of(down(block), down(block * block)))

    @pl.when(i == steps - 1)
    def _():
        tell(st_out, acc[...])


def ffn_kernel(
    steps, st, norm, gb, mask, block, ct, up, dn,
    out, gn_out, norm_out, st_out, gup_out, gdn_out,
    normed, normed_t, ct_t, branch, gn, coef,
):
    j = pl.program_id(0)

    @pl.when(j == 0)
    def _():
        sums = jnp.sum(st[...], axis=0)
        coef[...] = rows_of(*center(sums[0:1], sums[1:2], norm[2:3]))
        norm_out[...] = coef[...]
        scale = coef[1:2] * gb[4:5]
        shift = gb[9:10] - coef[0:1] * scale
        value = ((block[...] * scale + shift) * mask[...]).astype(BF16)
        normed[...] = value
        normed_t[...] = value.T
        ct_t[...] = ct[...].T
        branch[...] = jnp.zeros_like(branch)
        gn[...] = jnp.zeros_like(gn)

    hidden, slope = gelu_parts(dot(normed[...], up[0]))
    hidden = hidden.astype(BF16)
    branch[...] += dot_t(hidden, dn[0])
    gdn_out[0] = dot(ct_t[...], hidden).astype(BF16)
    grad = (slope * dot(ct[...], dn[0])).astype(BF16)
    gup_out[0] = dot(normed_t[...], grad).astype(BF16)
    gn[...] += dot_t(grad, up[0])

    @pl.when(j == steps - 1)
    def _():
        out[...] = (block[...] + branch[...]).astype(BF16)
        masked = gn[...] * mask[...]
        gn_out[...] = masked
        normal = (block[...] - coef[0:1]) * coef[1:2]
        tell(st_out, rows_of(down(masked), down(masked * normal)))


def merge_back_kernel(
    steps, st, norm, norm_two, norm_four, gb, mask, block, gn, ct, merged, large, small, w_out,
    gblock_out, gout_out, g_out, sums_out, st_out, coef, acc, gw,
):
    i = pl.program_id(0)

    @pl.when(i == 0)
    def _():
        coef[...] = jnp.sum(st[...], axis=0)
        sums_out[...] = coef[...]

    average, inverse = norm_four[0:1], norm_four[1:2]
    normal = (block[...] - average) * inverse
    here = mask[...]
    inside = gn[...] - (coef[0:1] + normal * coef[1:2]) / norm[2:3]
    gblock = ct[...].astype(F32) + here * (gb[4:5] * inverse * inside)
    gblock_out[...] = gblock
    branch = gblock.astype(BF16)
    add_up(gw, i, t_dot(merged[...], branch))
    v_large = (large[...] - norm_two[0:1]) * norm_two[1:2]
    v_small = (small[...] - norm_two[2:3]) * norm_two[3:4]
    pre = v_large * gb[2:3] + v_small * gb[3:4] + (gb[7:8] + gb[8:9])
    _, slope = gelu_parts(pre)
    g = here * slope * dot_t(branch, w_out[...])
    g_out[...] = g
    add_up(acc, i, rows_of(down(g), down(g * v_large), down(g * v_small)))

    @pl.when(i == steps - 1)
    def _():
        tell(st_out, acc[...])
        gout_out[...] = gw[...].astype(BF16)


def spread_back_kernel(
    images, st, norm, norm_one, norm_two, gb, mask, inner, large, small, g, moved, fourier, back,
    tap_large, tap_small, waves_large, waves_small, g_out, gk_out, sums_out, st_out,
):
    sums = jnp.sum(st[...], axis=0)
    sums_out[...] = sums
    pixels = norm[2:3]
    by_bias = sums[0:1] / pixels
    half = fourier.shape[0] // 2
    totals = None
    kernel_moved = [None, None]
    for n in range(images):
        rows = slice(n * SPOTS, (n + 1) * SPOTS)
        here = mask[rows]
        sc, ss = moved[n, :half], moved[n, half:]
        total_c = total_s = None
        for k, (value, tap) in enumerate(((large, tap_large), (small, tap_small))):
            average, inverse = norm_two[2 * k : 2 * k + 1], norm_two[2 * k + 1 : 2 * k + 2]
            normal = (value[rows] - average) * inverse
            inside = g[rows] - (by_bias + normal * (sums[1 + k : 2 + k] / pixels))
            gradient = (here * (gb[2 + k : 3 + k] * inverse * inside)).astype(BF16)
            change = dot(fourier[...], gradient)
            gc, gs = change[:half], change[half:]
            kc, ks = tap[:half], tap[half:]
            real, imag = gc * kc - gs * ks, gc * ks + gs * kc
            total_c = real if k == 0 else total_c + real
            total_s = imag if k == 0 else total_s + imag
            real, imag = sc * gc + ss * gs, ss * gc - sc * gs
            pair = kernel_moved[k]
            kernel_moved[k] = (real, imag) if n == 0 else (pair[0] + real, pair[1] + imag)
        both = jnp.concatenate([total_c.astype(BF16), total_s.astype(BF16)], axis=0)
        grad_spread = dot(back[...], both)
        normal = (inner[rows] - norm_one[0:1]) * norm_one[1:2]
        _, slope = gelu_parts(normal * gb[1:2] + gb[6:7])
        first = here * slope * grad_spread
        g_out[rows] = first
        part = rows_of(down(first), down(first * normal))
        totals = part if n == 0 else totals + part
    tell(st_out, totals)
    for k, table in enumerate((waves_large, waves_small)):
        real, imag = kernel_moved[k]
        both = jnp.concatenate([real.astype(BF16), imag.astype(BF16)], axis=0)
        width = waves_large.shape[1]
        place = slice(0, width) if k == 0 else slice(width, width + table.shape[1])
        gk_out[:, place] = t_dot(both, table[...]).astype(BF16)


def inner_back_kernel(
    steps, st, norm, norm_one, gb, mask, inner, g, first, x, w_in,
    gf_out, gin_out, sums_out, st_out, coef, acc, gw,
):
    i = pl.program_id(0)

    @pl.when(i == 0)
    def _():
        coef[...] = jnp.sum(st[...], axis=0)
        sums_out[...] = coef[...]

    average, inverse = norm_one[0:1], norm_one[1:2]
    normal = (inner[...] - average) * inverse
    here = mask[...]
    inside = g[...] - (coef[0:1] + normal * coef[1:2]) / norm[2:3]
    grad = (here * (gb[1:2] * inverse * inside)).astype(BF16)
    add_up(gw, i, t_dot(first[...], grad))
    gf = here * dot_t(grad, w_in[...])
    gf_out[...] = gf
    add_up(acc, i, rows_of(down(gf), down(gf * ((x[...] - norm[0:1]) * norm[1:2]))))

    @pl.when(i == steps - 1)
    def _():
        tell(st_out, acc[...])
        gin_out[...] = gw[...].astype(BF16)


def unmix_kernel(images, rel, ratio, st, norm, gb, mask, gblock, gf, x, target, own_out, prev_out, sums_out, prev, coef):
    i = pl.program_id(0)

    @pl.when(i == 0)
    def _():
        coef[...] = jnp.sum(st[...], axis=0)
        sums_out[...] = coef[...]
        prev[...] = jnp.zeros_like(prev)
        own_out[...] = jnp.zeros_like(own_out)

    normal = (x[0] - norm[0:1]) * norm[1:2]
    inside = gf[0] - (coef[0:1] + normal * coef[1:2]) / norm[2:3]
    grad = (mask[...] * (gblock[0] + gb[0:1] * norm[1:2] * inside)).astype(BF16)
    pick = (target[0] == lax.broadcasted_iota(jnp.int32, (SPOTS, SPOTS), 0)).astype(BF16)
    grad = dot(pick, grad)
    own_out[i] += ratio[i] * grad
    giving = (1.0 - ratio[i]) * grad
    to = rel[i]

    @pl.when(to < images)
    def _():
        prev[jnp.minimum(to, images - 1)] += giving

    @pl.when(to >= images)
    def _():
        own_out[jnp.maximum(to - images, 0)] += giving

    @pl.when(i == images - 1)
    def _():
        prev_out[...] = prev[...].astype(BF16)


def shape(dims, kind=F32):
    return jax.ShapeDtypeStruct(dims, kind)


def whole(dims):
    return pl.BlockSpec(dims, lambda *_: (0,) * len(dims))


def by_rows(rows, columns):
    return pl.BlockSpec((rows, columns), lambda i: (i, 0))


def params():
    return pltpu.CompilerParams(vmem_limit_bytes=VMEM)


def shifted(block, distance):
    count = lax.axis_size(BOTH)
    return lax.ppermute(block, BOTH, [((i - distance) % count, i) for i in range(count)])


def exchange(parts):
    return lax.all_to_all(parts, BOTH, 0, 0)


def shards(
    raw_maps, partner, ratios, offsets, flip_bits, size_class, proj_in, kernel_large, kernel_small,
    proj_out, norm_gain, norm_bias, ffn_up, ffn_down, cotangent,
):
    images, channels = raw_maps.shape[0], raw_maps.shape[3]
    share = proj_in.shape[0]
    count = lax.axis_size(BOTH)
    position = lax.axis_index(BOTH)
    pixels_here = images * SPOTS
    rows = pixels_here // STEPS
    large_extent, small_extent = kernel_large.shape[0], kernel_small.shape[0]
    large_taps, small_taps = large_extent**2, small_extent**2
    large_wide, small_wide = padded(large_taps), padded(small_taps)
    spots = [(r, c) for r in range(CANVAS) for c in range(CANVAS)]
    fourier_np = waves(spots, large_extent, SPOTS, False)
    fourier, back = jnp.asarray(fourier_np), jnp.asarray(np.ascontiguousarray(fourier_np.T))
    waves_large = jnp.asarray(waves(taps(large_extent), large_extent, large_wide, True))
    waves_small = jnp.asarray(waves(taps(small_extent), large_extent, small_wide, True))
    bins = fourier_np.shape[0]

    raw = raw_maps.reshape(images, SPOTS, channels)
    ct = cotangent.reshape(pixels_here, channels)
    earlier = shifted(raw, 1)

    norms = jnp.pad(jnp.concatenate([norm_gain, norm_bias], axis=0).T, ((0, 0), (0, 118)))
    early = exchange(jnp.broadcast_to(jnp.concatenate([proj_in, norms], axis=1)[None], (count, share, channels + 128)))
    early = early.reshape(channels, channels + 128)
    w_in = early[:, :channels]
    gb = early[:, channels : channels + 16].T.astype(F32)
    taps_here = jnp.concatenate(
        [
            jnp.pad(kernel_large.reshape(large_taps, share).T, ((0, 0), (0, large_wide - large_taps))),
            jnp.pad(kernel_small.reshape(small_taps, share).T, ((0, 0), (0, small_wide - small_taps))),
            proj_out,
        ],
        axis=1,
    )
    middle = lax.all_gather(taps_here, BOTH, axis=0, tiled=True)
    kt, w_out = middle[:, : large_wide + small_wide], middle[:, large_wide + small_wide :]
    hidden_here = ffn_up.shape[1]
    ffn_own = lax.all_gather(jnp.concatenate([ffn_up, ffn_down.T], axis=1), "batch", axis=0, tiled=True)
    swap = [(0, 1), (1, 0)]
    ffn = jnp.stack([ffn_own, lax.ppermute(ffn_own, "hid", swap)])

    sides = SMALL + (CANVAS - SMALL) * size_class
    spot = lax.broadcasted_iota(jnp.int32, (images, SPOTS), 1)
    row, column = spot // CANVAS, spot % CANVAS
    inside = (row < sides[:, None]) & (column < sides[:, None])
    corner = jnp.minimum(offsets, (CANVAS - sides)[:, None])
    source = column + corner[:, 1:2]
    source = jnp.where(flip_bits[:, None] > 0, CANVAS - 1 - source, source)
    target = jnp.where(inside, (row + corner[:, 0:1]) * CANVAS + source, -1)
    mask = inside.astype(F32).reshape(pixels_here, 1)
    relative = jnp.mod(partner - (position * images - images), count * images)

    def stats(k):
        return shape((count, k, channels)), whole((count, k, channels))

    def call(kernel, grid, ins, in_specs, outs, out_specs, scratch=(), prefetch=0):
        spec = pltpu.PrefetchScalarGridSpec(
            num_scalar_prefetch=prefetch, grid=grid, in_specs=in_specs, out_specs=out_specs, scratch_shapes=list(scratch)
        )
        return pl.pallas_call(kernel, grid_spec=spec, out_shape=outs, compiler_params=params())(*ins)

    row_c = by_rows(rows, channels)
    row_1 = by_rows(rows, 1)
    map_f = shape((pixels_here, channels))
    map_b = shape((pixels_here, channels), BF16)
    norm_spec = whole((3, channels))
    gb_spec = whole((16, channels))
    square = whole((channels, channels))
    image_spec = pl.BlockSpec((1, SPOTS, channels), lambda i, *_: (i, 0, 0))
    image_f = shape((images, SPOTS, channels))

    shape3, spec3 = stats(3)
    x, st = call(
        functools.partial(mix_kernel, images),
        (images,),
        (relative, ratios, sides, raw, earlier, raw, target[:, :, None]),
        [
            image_spec,
            pl.BlockSpec((1, SPOTS, channels), lambda i, rel, *_: (jnp.minimum(rel[i], images - 1), 0, 0)),
            pl.BlockSpec((1, SPOTS, channels), lambda i, rel, *_: (jnp.maximum(rel[i] - images, 0), 0, 0)),
            pl.BlockSpec((1, SPOTS, 1), lambda i, *_: (i, 0, 0)),
        ],
        (image_f, shape3),
        (image_spec, spec3),
        [pltpu.VMEM((SPOTS, channels), BF16), pltpu.VMEM((3, channels), F32)],
        prefetch=3,
    )
    x = x.reshape(pixels_here, channels)
    st = exchange(st)

    shape2, spec2 = stats(2)
    first, inner, norm, st = call(
        functools.partial(inner_kernel, STEPS),
        (STEPS,),
        (st, gb, mask, x, w_in),
        [spec3, gb_spec, row_1, row_c, square],
        (map_b, map_f, shape((3, channels)), shape2),
        (row_c, row_c, norm_spec, spec2),
        [pltpu.VMEM((3, channels), F32), pltpu.VMEM((2, channels), F32)],
    )
    st = exchange(st)

    chunk = 256 if channels % 256 == 0 else channels
    chunks = channels // chunk
    tap_shape = shape((bins, channels))
    tap_spec = pl.BlockSpec((bins, chunk), lambda i: (0, i))
    kt_spec = pl.BlockSpec((chunk, large_wide + small_wide), lambda i: (i, 0))
    wl_spec, ws_spec = whole((bins, large_wide)), whole((bins, small_wide))
    tap_large, tap_small = call(
        taps_kernel,
        (chunks,),
        (kt, waves_large, waves_small),
        [kt_spec, wl_spec, ws_spec],
        (tap_shape, tap_shape),
        (tap_spec, tap_spec),
    )

    def chunk_stats(k):
        return pl.BlockSpec((count, k, chunk), lambda i: (0, 0, i))

    def chunk_rows(k):
        return pl.BlockSpec((k, chunk), lambda i: (0, i))

    four_spec, back_spec = whole((bins, SPOTS)), whole((SPOTS, bins))
    mask_spec = whole((pixels_here, 1))
    shape4, spec4 = stats(4)
    moved_spec = pl.BlockSpec((images, bins, chunk), lambda i: (0, 0, i))
    large, small, moved, norm_one, st = call(
        functools.partial(spread_kernel, images),
        (chunks,),
        (st, norm, gb, mask, inner, fourier, back, tap_large, tap_small),
        [chunk_stats(2), chunk_rows(3), chunk_rows(16), mask_spec, chunk_rows(pixels_here), four_spec, back_spec, tap_spec, tap_spec],
        (map_f, map_f, shape((images, bins, channels)), shape((2, channels)), shape4),
        (chunk_rows(pixels_here), chunk_rows(pixels_here), moved_spec, chunk_rows(2), chunk_stats(4)),
    )
    st = exchange(st)

    merged, block, norm_two, st = call(
        functools.partial(merge_kernel, STEPS),
        (STEPS,),
        (st, norm, gb, mask, large, small, x, w_out),
        [spec4, norm_spec, gb_spec, row_1, row_c, row_c, row_c, square],
        (map_b, map_f, shape((4, channels)), shape2),
        (row_c, row_c, whole((4, channels)), spec2),
        [pltpu.VMEM((4, channels), F32), pltpu.VMEM((2, channels), F32)],
    )
    st = exchange(st)

    wide = 256 if hidden_here % 256 == 0 else hidden_here
    per_half = hidden_here // wide
    steps = 2 * per_half
    map_spec = whole((pixels_here, channels))
    up_spec = pl.BlockSpec((1, channels, wide), lambda j: (j // per_half, 0, j % per_half))
    dn_spec = pl.BlockSpec((1, channels, wide), lambda j: (j // per_half, 0, per_half + j % per_half))
    gw_shape = shape((2, channels, hidden_here), BF16)
    output, gn, norm_four, st, gup, gdn = call(
        functools.partial(ffn_kernel, steps),
        (steps,),
        (st, norm, gb, mask, block, ct, ffn, ffn),
        [spec2, norm_spec, gb_spec, mask_spec, map_spec, map_spec, up_spec, dn_spec],
        (map_b, map_f, shape((2, channels)), shape2, gw_shape, gw_shape),
        (map_spec, map_spec, whole((2, channels)), spec2, up_spec, up_spec),
        [
            pltpu.VMEM((pixels_here, channels), BF16),
            pltpu.VMEM((channels, pixels_here), BF16),
            pltpu.VMEM((channels, pixels_here), BF16),
            pltpu.VMEM((pixels_here, channels), F32),
            pltpu.VMEM((pixels_here, channels), F32),
            pltpu.VMEM((2, channels), F32),
        ],
    )
    st = exchange(st)
    gffn_other = jnp.concatenate([gup[1], gdn[1]], axis=1)
    gffn = jnp.concatenate([gup[0], gdn[0]], axis=1).astype(F32)
    gffn = (gffn + lax.ppermute(gffn_other, "hid", swap).astype(F32)).astype(BF16)
    gffn = lax.psum_scatter(gffn, "batch", scatter_dimension=0, tiled=True).astype(F32)

    gw_here = shape((channels, channels), BF16)
    gblock, gout, g, sums_four, st = call(
        functools.partial(merge_back_kernel, STEPS),
        (STEPS,),
        (st, norm, norm_two, norm_four, gb, mask, block, gn, ct, merged, large, small, w_out),
        [spec2, norm_spec, whole((4, channels)), whole((2, channels)), gb_spec, row_1] + [row_c] * 6 + [square],
        (map_f, gw_here, map_f, shape((2, channels)), shape3),
        (row_c, square, row_c, whole((2, channels)), spec3),
        [pltpu.VMEM((2, channels), F32), pltpu.VMEM((3, channels), F32), pltpu.VMEM((channels, channels), F32)],
    )
    st = exchange(st)

    gk_shape = shape((channels, large_wide + small_wide), BF16)
    map_chunk = chunk_rows(pixels_here)
    g, gk, sums_two, st = call(
        functools.partial(spread_back_kernel, images),
        (chunks,),
        (st, norm, norm_one, norm_two, gb, mask, inner, large, small, g, moved, fourier, back, tap_large, tap_small, waves_large, waves_small),
        [chunk_stats(3), chunk_rows(3), chunk_rows(2), chunk_rows(4), chunk_rows(16), mask_spec, map_chunk, map_chunk, map_chunk, map_chunk,
         moved_spec, four_spec, back_spec, tap_spec, tap_spec, wl_spec, ws_spec],
        (map_f, gk_shape, shape((3, channels)), shape2),
        (map_chunk, kt_spec, chunk_rows(3), chunk_stats(2)),
    )
    st = exchange(st)
    gmiddle = jnp.concatenate([gk, gout], axis=1).reshape(count, share, large_wide + small_wide + channels)
    gmiddle = jnp.sum(exchange(gmiddle).astype(F32), axis=0)

    gf, gin, sums_one, st = call(
        functools.partial(inner_back_kernel, STEPS),
        (STEPS,),
        (st, norm, norm_one, gb, mask, inner, g, first, x, w_in),
        [spec2, norm_spec, whole((2, channels)), gb_spec, row_1, row_c, row_c, row_c, row_c, square],
        (map_f, gw_here, shape((2, channels)), shape2),
        (row_c, square, whole((2, channels)), spec2),
        [pltpu.VMEM((2, channels), F32), pltpu.VMEM((2, channels), F32), pltpu.VMEM((channels, channels), F32)],
    )
    st = exchange(st)
    gin = jnp.sum(exchange(gin.reshape(count, share, channels)).astype(F32), axis=0)

    all_images = whole((images, SPOTS, channels))
    own, prev, sums_zero = call(
        functools.partial(unmix_kernel, images),
        (images,),
        (
            relative, ratios, st, norm, gb, mask, gblock.reshape(images, SPOTS, channels),
            gf.reshape(images, SPOTS, channels), x.reshape(images, SPOTS, channels), target[:, None, :],
        ),
        [
            spec2, norm_spec, gb_spec, pl.BlockSpec((SPOTS, 1), lambda i, *_: (i, 0)), image_spec, image_spec, image_spec,
            pl.BlockSpec((1, 1, SPOTS), lambda i, *_: (i, 0, 0)),
        ],
        (image_f, shape((images, SPOTS, channels), BF16), shape((2, channels))),
        (all_images, all_images, whole((2, channels))),
        [pltpu.VMEM((images, SPOTS, channels), F32), pltpu.VMEM((2, channels), F32)],
        prefetch=2,
    )
    grad_raw = own + shifted(prev, -1).astype(F32)

    gains = jnp.concatenate([sums_zero[1:2], sums_one[1:2], sums_two[1:3], sums_four[1:2]], axis=0)
    biases = jnp.concatenate([sums_zero[0:1], sums_one[0:1], sums_two[0:1], sums_two[0:1], sums_four[0:1]], axis=0)
    canvas = (images, CANVAS, CANVAS, channels)
    return (
        output.reshape(canvas),
        grad_raw.reshape(canvas),
        gin,
        gmiddle[:, :large_taps].T.reshape(large_extent, large_extent, share),
        gmiddle[:, large_wide : large_wide + small_taps].T.reshape(small_extent, small_extent, share),
        gmiddle[:, large_wide + small_wide :],
        lax.dynamic_slice_in_dim(gains, position * share, share, 1),
        lax.dynamic_slice_in_dim(biases, position * share, share, 1),
        gffn[:, :hidden_here],
        gffn[:, hidden_here:].T,
    )


def solution(mesh):
    one = P(BOTH)
    maps = P(BOTH, None, None, None)
    flat = P(BOTH, None)
    kernels = P(None, None, BOTH)
    norms = P(None, BOTH)
    return jax.shard_map(
        shards,
        mesh=mesh,
        in_specs=(
            maps, one, one, flat, one, one, flat, kernels, kernels, flat, norms, norms,
            P("batch", "hid"), P("hid", "batch"), maps,
        ),
        out_specs=(maps, maps, flat, kernels, kernels, flat, norms, norms, P("batch", "hid"), P("hid", "batch")),
        check_vma=False,
    )
```

time: 2270 us -> 438 us (0.19)
  matrix products: 1160 us -> 0 us
  blocking collectives: 578 us -> 47.5 us
  local copies, waits for them, and re-layouts: 213 us -> 22.8 us
  Pallas kernels: 0 us -> 115 us
  other arithmetic: 77 us -> 24.9 us
  waiting for transfers between devices: 211 us -> 180 us
  starting transfers between devices: 3.86 us -> 31.5 us
    conv_general_dilated x6 -> x0, matrix products: 1080 us -> none  [the longest x2 722 us: kernel_grad(): lax.conv_general_dilated(spread, gradient, (1, 1), ((radius, radius), (ra...]
    psum x8 -> x0, blocking collectives: 322 us -> none  [the longest x4 162 us: norm_back(): by_bias, by_gain = lax.psum((by_bias, by_gain), ('batch', 'hid'))]
    all_gather x6 -> x0, blocking collectives: 256 us -> none  [the longest x1 50.7 us: shards(): lax.all_gather(kernel_large, ('batch', 'hid'), axis=2, tiled=True)]
    pallas_call x0 -> x10, Pallas kernels: none -> 115 us  [call(): pl.pallas_call(kernel, grid_spec=spec, out_shape=outs, compiler_params=pa...]
    reduce_scatter x7 -> x1, waiting for transfers between devices: 132 us -> 31.2 us  [shards(): lax.psum_scatter(gffn, 'batch', scatter_dimension=0, tiled=True).astype(F32)]
    dot_general x14 -> x0, matrix products: 77.3 us -> none  [the longest x1 11.6 us: shards(): jnp.einsum('nhwc,cf->nhwf', rows_in, up_half, preferred_element_type=jnp....]
    scatter-add x10 -> x0, local copies, waits for them, and re-layouts: 75.9 us -> none
    all_to_all x0 -> x4, blocking collectives: none -> 47.5 us  [exchange(): return lax.all_to_all(parts, BOTH, 0, 0)]
  transfers between devices with their start and end apart: 14 -> 14, of which waited for: 6 -> 8; matrix products, arithmetic and copies ran while one was open for 63% -> 8% of each run, Pallas kernels for 0% -> 20%
where the time goes in v1:
time: 438 us; the launch traced here: 436 us
  waiting for transfers between devices  180 us (41%)
  Pallas kernels  115 us (26%)
  blocking collectives  47.5 us (11%)
  starting transfers between devices  31.5 us (7%)
  other arithmetic  24.9 us (6%)
  local copies, waits for them, and re-layouts  22.8 us (5%)
  between operations  14.1 us (3%)
    pallas_call x10, Pallas kernels, call(): pl.pallas_call(kernel, grid_spec=spec, out_shape=outs, compiler_params=pa...  115 us
    all_gather x1, waiting for transfers between devices, shards(): lax.all_gather(jnp.concatenate([ffn_up, ffn_down.T], axis=1), 'batch', ax...  63.2 us
    all_to_all x4, blocking collectives, exchange(): return lax.all_to_all(parts, BOTH, 0, 0)  47.5 us
    reduce_scatter x1, waiting for transfers between devices, shards(): lax.psum_scatter(gffn, 'batch', scatter_dimension=0, tiled=True).astype(F32)  31.2 us
    all_to_all x7, waiting for transfers between devices, exchange(): return lax.all_to_all(parts, BOTH, 0, 0)  30.3 us
    ppermute x2, waiting for transfers between devices, shifted(): lax.ppermute(block, BOTH, [((i - distance) % count, i) for i in range(cou...  30.1 us
    all_to_all x7, starting transfers between devices, exchange(): return lax.all_to_all(parts, BOTH, 0, 0)  25.4 us
    all_gather x1, waiting for transfers between devices, shards(): middle = lax.all_gather(taps_here, BOTH, axis=0, tiled=True)  24.8 us
  transfers between devices with their start and end apart: 14, of which 8 were waited for; matrix products, arithmetic and copies ran while one was open for 8% of the time, Pallas kernels for 20%

profile of v1, /device:TPU:0, one launch (start us, length us, event | category | flops | bytes accessed | tf_op | source)
XLA Modules:
  0.0 435.9 jit_solution(10927866416108510833)
XLA Ops:
  7.3 1.5 pad_maximum_fusion.3
  8.9 0.9 copy.38
  10.8 1.3 fusion.8
  14.2 0.9 broadcast_in_dim.30
  15.1 7.1 %all-to-all-start.1 = ((bf16[32,16,640]{2,1,0:T(8,128)(2,1)}), bf16[32,16,640]{2,1,0:T(8,128)(2,1)S(1)}, u32[]{:S(2)}, u32[]{:S(2)}) async-start(bf16[32,16,640]{2,1,0:T(8,128)(2,1)} %broadcast_in_dim.30), calls=%async_computation.1 | async-start | bytes 1310720 | tf_op jit(solution)/shard_map/all_to_all | solution.py:417
  22.9 63.2 %all-gather.5.cloned.1.call-done = bf16[512,2048]{1,0:T(8,128)(2,1)} async-done(((bf16[32,2048]{1,0:T(8,128)(2,1)}), bf16[512,2048]{1,0:T(8,128)(2,1)}) %all-gather.5.cloned.1.call-update) | async-done | bytes 2097168 | tf_op jit(solution)/shard_map/all_gather | solution.py:460
  86.3 1.4 fusion.2.target
  87.8 1.0 copy-done.2
  88.8 6.5 %shard_map.258 = (f32[2,576,512]{2,1,0:T(8,128)}, f32[32,3,512]{2,1,0:T(4,128)}) custom-call(s32[2]{0:T(128)} %get-tuple-element.118.rel, f32[2]{0:T(128)} %ratio.3, s32[2]{0:T(128)} %copy-done.10, bf16[2,576,512]{2,1,0:T(8,128)(2,1)} %bitcast.41, bf16[2,576,512]{2,1,0:T(8,128)(2,1)} %copy-done.2, bf16[2,576,512]{2,1,0:T(8,128)(2,1)} %bitcast.42, ...), custom_call_target="tpu_custom_call" | custom-call | tf_op jit(solution)/shard_map/pallas_call | solution.py:482
  95.3 3.6 all-to-all-start
  99.5 1.3 reshape.695.mask
  102.3 7.8 %all-to-all-done.st = f32[32,3,512]{2,1,0:T(4,128)S(1)} async-done(((f32[32,3,512]{2,1,0:T(4,128)}), f32[32,3,512]{2,1,0:T(4,128)S(1)}, u32[]{:S(2)}, u32[]{:S(2)}) %all-to-all-start) | async-done | bytes 196640 | tf_op jit(solution)/shard_map/all_to_all | solution.py:417
  110.9 5.4 %shard_map.259 = (bf16[1152,512]{1,0:T(8,128)(2,1)}, f32[1152,512]{1,0:T(8,128)}, f32[3,512]{1,0:T(4,128)}, f32[32,2,512]{2,1,0:T(2,128)}) custom-call(f32[32,3,512]{2,1,0:T(4,128)} %copy-done.3, f32[16,512]{1,0:T(8,128)} %convert_bitcast_fusion.gb, f32[1152,1]{1,0:T(8,128)} %reshape.695.mask, f32[1152,512]{1,0:T(8,128)} %bitcast.37, ...), custom_call_target="tpu_custom_call" | custom-call | tf_op jit(solution)/shard_map/pallas_call | solution.py:482
  116.3 2.6 all-to-all-start.2
  118.9 24.8 %all-gather.3.cloned.1.call-done = bf16[512,1408]{1,0:T(8,128)(2,1)} async-done(((bf16[16,1408]{1,0:T(8,128)(2,1)}), bf16[512,1408]{1,0:T(8,128)(2,1)}) %all-gather.3.cloned.1.call-update) | async-done | bytes 1441808 | tf_op jit(solution)/shard_map/all_gather | solution.py:457
  143.7 2.2 slice.95.kt
  145.9 5.3 %shard_map.260 = (f32[1376,512]{1,0:T(8,128)}, f32[1376,512]{1,0:T(8,128)}) custom-call(bf16[512,896]{1,0:T(8,128)(2,1)} %slice.95.kt, bf16[1376,768]{1,0:T(8,128)(2,1)} %constant.75.clone.waves_large, bf16[1376,128]{1,0:T(8,128)(2,1)} %constant.76.clone.waves_small), custom_call_target="tpu_custom_call" | custom-call | tf_op jit(solution)/shard_map/pallas_call | solution.py:482
  151.8 13.8 %shard_map.261 = (f32[1152,512]{1,0:T(8,128)}, f32[1152,512]{1,0:T(8,128)}, f32[2,1376,512]{2,1,0:T(8,128)}, f32[2,512]{1,0:T(2,128)}, f32[32,4,512]{2,1,0:T(4,128)}) custom-call(f32[32,2,512]{2,1,0:T(2,128)} %copy-done.6, f32[3,512]{1,0:T(4,128)} %get-tuple-element.52.norm, f32[16,512]{1,0:T(8,128)} %convert_bitcast_fusion.gb, f32[1152,1]{1,0:T(8,128)} %reshape.695.mask, ...), custom_call_target="tpu_custom_call" | custom-call | tf_op jit(solution)/shard_map/pallas_call | solution.py:482
  165.6 3.6 all-to-all-start.3
  169.2 1.9 slice.96.w_out
  171.1 8.7 %all-to-all-done.3.st = f32[32,4,512]{2,1,0:T(4,128)S(1)} async-done(((f32[32,4,512]{2,1,0:T(4,128)}), f32[32,4,512]{2,1,0:T(4,128)S(1)}, u32[]{:S(2)}, u32[]{:S(2)}) %all-to-all-start.3) | async-done | bytes 262176 | tf_op jit(solution)/shard_map/all_to_all | solution.py:417
  180.5 7.1 %shard_map.262 = (bf16[1152,512]{1,0:T(8,128)(2,1)}, f32[1152,512]{1,0:T(8,128)}, f32[4,512]{1,0:T(4,128)}, f32[32,2,512]{2,1,0:T(2,128)}) custom-call(f32[32,4,512]{2,1,0:T(4,128)} %copy-done.4, f32[3,512]{1,0:T(4,128)} %get-tuple-element.52.norm, f32[16,512]{1,0:T(8,128)} %convert_bitcast_fusion.gb, f32[1152,1]{1,0:T(8,128)} %reshape.695.mask, ...), custom_call_target="tpu_custom_call" | custom-call | tf_op jit(solution)/shard_map/pallas_call | solution.py:482
  187.6 2.8 all-to-all-start.4
  190.4 4.0 pad_maximum_fusion.up.dn
  194.4 4.0 all-to-all-done.4.st
  199.1 29.0 %shard_map.263 = (bf16[1152,512]{1,0:T(8,128)(2,1)}, f32[1152,512]{1,0:T(8,128)}, f32[2,512]{1,0:T(2,128)}, f32[32,2,512]{2,1,0:T(2,128)}, bf16[2,512,1024]{2,1,0:T(8,128)(2,1)}, /*index=5*/bf16[2,512,1024]{2,1,0:T(8,128)(2,1)}) custom-call(f32[32,2,512]{2,1,0:T(2,128)} %copy-done.7, f32[3,512]{1,0:T(4,128)} %get-tuple-element.52.norm, ...), custom_call_target="tpu_custom_call" | custom-call | tf_op jit(solution)/shard_map/pallas_call | solution.py:482
  228.1 1.9 slice_bitcast_fusion.3
  230.5 1.5 pad_maximum_fusion.1
  232.2 10.6 %all_to_all.55.st = f32[32,2,512]{2,1,0:T(2,128)} all-to-all(f32[32,2,512]{2,1,0:T(2,128)S(1)} %copy-done.9), channel_id=1, replica_groups=mesh['batch'=16,'hid'=2] {'batch','hid'}, dimensions={0} | all-to-all | bytes 262144 | tf_op jit(solution)/shard_map/all_to_all | solution.py:417
  242.8 11.0 %shard_map.264 = (f32[1152,512]{1,0:T(8,128)}, bf16[512,512]{1,0:T(8,128)(2,1)}, f32[1152,512]{1,0:T(8,128)}, f32[2,512]{1,0:T(2,128)}, f32[32,3,512]{2,1,0:T(4,128)}) custom-call(f32[32,2,512]{2,1,0:T(2,128)} %all_to_all.55.st, f32[3,512]{1,0:T(4,128)} %get-tuple-element.52.norm, f32[4,512]{1,0:T(4,128)} %get-tuple-element.63.norm_two, ...), custom_call_target="tpu_custom_call" | custom-call | tf_op jit(solution)/shard_map/pallas_call | solution.py:482
  253.8 13.9 %all_to_all.56.st = f32[32,3,512]{2,1,0:T(4,128)} all-to-all(f32[32,3,512]{2,1,0:T(4,128)} %get-tuple-element.67), channel_id=1, replica_groups=mesh['batch'=16,'hid'=2] {'batch','hid'}, dimensions={0} | all-to-all | bytes 393216 | tf_op jit(solution)/shard_map/all_to_all | solution.py:417
  267.7 21.0 %shard_map.265 = (f32[1152,512]{1,0:T(8,128)}, bf16[512,896]{1,0:T(8,128)(2,1)}, f32[3,512]{1,0:T(4,128)}, f32[32,2,512]{2,1,0:T(2,128)}) custom-call(f32[32,3,512]{2,1,0:T(4,128)} %all_to_all.56.st, f32[3,512]{1,0:T(4,128)} %get-tuple-element.52.norm, f32[2,512]{1,0:T(2,128)} %get-tuple-element.68.norm_one, f32[4,512]{1,0:T(4,128)} %get-tuple-element.63.norm_two, ...), custom_call_target="tpu_custom_call" | custom-call | tf_op jit(solution)/shard_map/pallas_call | solution.py:482
  288.7 11.5 %all_to_all.57.st = f32[32,2,512]{2,1,0:T(2,128)} all-to-all(f32[32,2,512]{2,1,0:T(2,128)} %get-tuple-element.71), channel_id=1, replica_groups=mesh['batch'=16,'hid'=2] {'batch','hid'}, dimensions={0} | all-to-all | bytes 262144 | tf_op jit(solution)/shard_map/all_to_all | solution.py:417
  300.2 8.3 %shard_map.266 = (f32[1152,512]{1,0:T(8,128)}, bf16[512,512]{1,0:T(8,128)(2,1)}, f32[2,512]{1,0:T(2,128)}, f32[32,2,512]{2,1,0:T(2,128)}) custom-call(f32[32,2,512]{2,1,0:T(2,128)} %all_to_all.57.st, f32[3,512]{1,0:T(4,128)} %get-tuple-element.52.norm, f32[2,512]{1,0:T(2,128)} %get-tuple-element.68.norm_one, f32[16,512]{1,0:T(8,128)} %convert_bitcast_fusion.gb, ...), custom_call_target="tpu_custom_call" | custom-call | tf_op jit(solution)/shard_map/pallas_call | solution.py:482
  308.5 11.5 %all_to_all.58.st = f32[32,2,512]{2,1,0:T(2,128)} all-to-all(f32[32,2,512]{2,1,0:T(2,128)} %get-tuple-element.74), channel_id=1, replica_groups=mesh['batch'=16,'hid'=2] {'batch','hid'}, dimensions={0} | all-to-all | bytes 262144 | tf_op jit(solution)/shard_map/all_to_all | solution.py:417
  320.1 2.6 all-to-all-start.9
  322.7 3.8 add_convert_fusion
  326.6 1.2 copy-done.5
  327.9 1.2 pad_maximum_fusion.2
  329.1 9.7 %all-to-all-done.9 = bf16[32,16,512]{2,1,0:T(8,128)(2,1)S(1)} async-done(((bf16[32,16,512]{2,1,0:T(8,128)(2,1)}), bf16[32,16,512]{2,1,0:T(8,128)(2,1)S(1)}, u32[]{:S(2)}, u32[]{:S(2)}) %all-to-all-start.9) | async-done | bytes 524320 | tf_op jit(solution)/shard_map/all_to_all | solution.py:417
  338.8 3.2 all-to-all-start.10
  342.7 8.1 %shard_map.267 = (f32[2,576,512]{2,1,0:T(8,128)}, bf16[2,576,512]{2,1,0:T(8,128)(2,1)}, f32[2,512]{1,0:T(2,128)}) custom-call(s32[2]{0:T(128)} %get-tuple-element.118.rel, f32[2]{0:T(128)} %ratio.3, f32[32,2,512]{2,1,0:T(2,128)} %all_to_all.58.st, f32[3,512]{1,0:T(4,128)} %get-tuple-element.52.norm, f32[16,512]{1,0:T(8,128)} %convert_bitcast_fusion.gb, ...), custom_call_target="tpu_custom_call" | custom-call | tf_op jit(solution)/shard_map/pallas_call | solution.py:482
  350.8 5.2 %collective-permute-start.2 = (bf16[2,576,512]{2,1,0:T(8,128)(2,1)}, bf16[2,576,512]{2,1,0:T(8,128)(2,1)S(1)}, u32[]{:S(2)}, u32[]{:S(2)}) collective-permute-start(bf16[2,576,512]{2,1,0:T(8,128)(2,1)} %get-tuple-element.78), channel_id=1, source_target_pairs={{1,0},{2,1},{3,2},{4,3},{5,4},{6,5},{7,6},{8,7},{9,8},{10,9},{11,1... | collective-permute-start | bytes 3538952 | tf_op jit(solution)/shard_map/ppermute | solution.py:413
  358.9 30.1 %collective-permute-done.2 = bf16[2,576,512]{2,1,0:T(8,128)(2,1)S(1)} collective-permute-done((bf16[2,576,512]{2,1,0:T(8,128)(2,1)}, bf16[2,576,512]{2,1,0:T(8,128)(2,1)S(1)}, u32[]{:S(2)}, u32[]{:S(2)}) %collective-permute-start.2) | collective-permute-done | bytes 1179680 | tf_op jit(solution)/shard_map/ppermute | solution.py:413
  388.9 3.5 convert_add_fusion
  395.0 31.2 %reduce-scatter.2.cloned.1.call-done = bf16[32,2048]{1,0:T(8,128)(2,1)} async-done(((bf16[512,2048]{1,0:T(8,128)(2,1)}), bf16[32,2048]{1,0:T(8,128)(2,1)}) %reduce-scatter.2.cloned.1.call-update) | async-done | bytes 131088 | tf_op jit(solution)/shard_map/reduce_scatter | solution.py:598
  426.2 0.9 convert_element_type.51
  427.8 1.5 slice.100
  (89 shorter events, 16.7 us)
Async XLA Ops:
  7.2 15.1 %copy-start.17 = (s32[2]{0:T(128)S(1)}, s32[2]{0:T(128)}, u32[]{:S(2)}) copy-start(s32[2]{0:T(128)} %param.20) | copy-start | bytes 28
  7.2 15.1 %copy-start.16 = (s32[2]{0:T(128)S(1)}, s32[2]{0:T(128)}, u32[]{:S(2)}) copy-start(s32[2]{0:T(128)} %param.24) | copy-start | bytes 28
  7.2 15.6 %copy-start.15 = (s32[2,2]{1,0:T(2,128)S(1)}, s32[2,2]{1,0:T(2,128)}, u32[]{:S(2)}) copy-start(s32[2,2]{1,0:T(2,128)} %param.22) | copy-start | bytes 52
  7.2 79.1 %copy-start.18 = (s32[2]{0:T(128)S(1)}, s32[2]{0:T(128)}, u32[]{:S(2)}) copy-start(s32[2]{0:T(128)} %param.23) | copy-start | bytes 28
  7.2 78.9 %all-gather.5.cloned.1.call-start = ((), (), s32[]{:S(2)}) async-start(), calls=%async_computation.13 | async-start | bytes 2228224 | tf_op jit(solution)/shard_map/all_gather | solution.py:460
  8.8 134.9 %all-gather.3.cloned.1.call-start = ((), (), s32[]{:S(2)}) async-start(), calls=%async_computation.12 | async-start | bytes 1486848 | tf_op jit(solution)/shard_map/all_gather | solution.py:457
  12.2 75.6 %collective-permute-start = (bf16[2,576,512]{2,1,0:T(8,128)(2,1)}, bf16[2,576,512]{2,1,0:T(8,128)(2,1)S(1)}, u32[]{:S(2)}, u32[]{:S(2)}) collective-permute-start(bf16[2,576,512]{2,1,0:T(8,128)(2,1)} %bitcast.40), channel_id=1, source_target_pairs={{31,0},{0,1},{1,2},{2,3},{3,4},{4,5},{5,6},{6,7},{7,8},{8,9},{9,10... | collective-permute-start | bytes 3538952 | tf_op jit(solution)/shard_map/ppermute | solution.py:413
  15.1 80.2 %all-to-all-start.1 = ((bf16[32,16,640]{2,1,0:T(8,128)(2,1)}), bf16[32,16,640]{2,1,0:T(8,128)(2,1)S(1)}, u32[]{:S(2)}, u32[]{:S(2)}) async-start(bf16[32,16,640]{2,1,0:T(8,128)(2,1)} %broadcast_in_dim.30), calls=%async_computation.1 | async-start | bytes 1310720 | tf_op jit(solution)/shard_map/all_to_all | solution.py:417
  22.8 65.0 %copy-start.10 = (s32[2]{0:T(128)}, s32[2]{0:T(128)S(1)}, u32[]{:S(2)}) copy-start(s32[2]{0:T(128)S(1)} %get-tuple-element.111.sides) | copy-start | bytes 28
  86.1 104.3 %collective-permute-start.1 = (bf16[512,2048]{1,0:T(8,128)(2,1)}, bf16[512,2048]{1,0:T(8,128)(2,1)}, u32[]{:S(2)}, u32[]{:S(2)}) collective-permute-start(bf16[512,2048]{1,0:T(8,128)(2,1)} %all-gather.5.cloned.1.call-done), channel_id=1, source_target_pairs={{0,1},{1,0},{2,3},{3,2},{4,5},{5,4},{6,7},{7,6},{8,9},{9,8},{10,11... | collective-permute-start | bytes 6291464 | tf_op jit(solution)/shard_map/ppermute | solution.py:462
  87.8 1.0 copy-start.2
  95.3 14.9 %all-to-all-start = ((f32[32,3,512]{2,1,0:T(4,128)}), f32[32,3,512]{2,1,0:T(4,128)S(1)}, u32[]{:S(2)}, u32[]{:S(2)}) async-start(f32[32,3,512]{2,1,0:T(4,128)} %get-tuple-element.49), calls=%async_computation | async-start | bytes 524288 | tf_op jit(solution)/shard_map/all_to_all | solution.py:417
  110.2 0.7 copy-start.3
  116.3 34.8 %all-to-all-start.2 = ((f32[32,2,512]{2,1,0:T(2,128)}), f32[32,2,512]{2,1,0:T(2,128)S(1)}, u32[]{:S(2)}, u32[]{:S(2)}) async-start(f32[32,2,512]{2,1,0:T(2,128)} %get-tuple-element.51), calls=%async_computation.2 | async-start | bytes 262144 | tf_op jit(solution)/shard_map/all_to_all | solution.py:417
  151.1 0.7 copy-start.6
  165.6 14.2 %all-to-all-start.3 = ((f32[32,4,512]{2,1,0:T(4,128)}), f32[32,4,512]{2,1,0:T(4,128)S(1)}, u32[]{:S(2)}, u32[]{:S(2)}) async-start(f32[32,4,512]{2,1,0:T(4,128)} %get-tuple-element.56), calls=%async_computation.3 | async-start | bytes 524288 | tf_op jit(solution)/shard_map/all_to_all | solution.py:417
  179.8 0.7 copy-start.4
  180.5 9.9 %copy-start.1 = (bf16[512,2048]{1,0:T(8,128)(2,1)S(1)}, bf16[512,2048]{1,0:T(8,128)(2,1)}, u32[]{:S(2)}) copy-start(bf16[512,2048]{1,0:T(8,128)(2,1)} %all-gather.5.cloned.1.call-done) | copy-start | bytes 6291460
  187.6 10.8 %all-to-all-start.4 = ((f32[32,2,512]{2,1,0:T(2,128)}), f32[32,2,512]{2,1,0:T(2,128)S(1)}, u32[]{:S(2)}, u32[]{:S(2)}) async-start(f32[32,2,512]{2,1,0:T(2,128)} %get-tuple-element.59), calls=%async_computation.4 | async-start | bytes 262144 | tf_op jit(solution)/shard_map/all_to_all | solution.py:417
  198.4 0.7 copy-start.7
  228.1 2.2 copy-start
  230.5 1.7 copy-start.9
  232.0 90.7 %collective-permute-start.3 = (bf16[512,2048]{1,0:T(8,128)(2,1)}, bf16[512,2048]{1,0:T(8,128)(2,1)}, u32[]{:S(2)}, u32[]{:S(2)}) collective-permute-start(bf16[512,2048]{1,0:T(8,128)(2,1)} %pad_maximum_fusion.1), channel_id=1, source_target_pairs={{0,1},{1,0},{2,3},{3,2},{4,5},{5,4},{6,7},{7,6},{8,9},{9,8},{10,11... | collective-permute-start | bytes 6291464 | tf_op jit(solution)/shard_map/ppermute | solution.py:597
  320.1 18.7 %all-to-all-start.9 = ((bf16[32,16,512]{2,1,0:T(8,128)(2,1)}), bf16[32,16,512]{2,1,0:T(8,128)(2,1)S(1)}, u32[]{:S(2)}, u32[]{:S(2)}) async-start(bf16[32,16,512]{2,1,0:T(8,128)(2,1)} %bitcast.51), calls=%async_computation.9 | async-start | bytes 1048576 | tf_op jit(solution)/shard_map/all_to_all | solution.py:417
  322.7 103.6 %reduce-scatter.2.cloned.1.call-start = ((), (), s32[]{:S(2)}) async-start(), calls=%async_computation.14 | async-start | bytes 2228224 | tf_op jit(solution)/shard_map/reduce_scatter | solution.py:598
  326.5 1.2 copy-start.5
  326.5 1.3 copy-start.8
  329.1 12.9 %copy-start.11 = (s32[2]{0:T(128)S(1)}, s32[2]{0:T(128)}, u32[]{:S(2)}) copy-start(s32[2]{0:T(128)} %copy-done.10) | copy-start | bytes 28
  338.8 53.6 %all-to-all-start.10 = ((bf16[32,16,1408]{2,1,0:T(8,128)(2,1)}), bf16[32,16,1408]{2,1,0:T(8,128)(2,1)S(1)}, u32[]{:S(2)}, u32[]{:S(2)}) async-start(bf16[32,16,1408]{2,1,0:T(8,128)(2,1)} %bitcast.16), calls=%async_computation.10 | async-start | bytes 2883584 | tf_op jit(solution)/shard_map/all_to_all | solution.py:417
  342.7 13.3 %copy-start.13 = (f32[2,512]{1,0:T(2,128)S(1)}, f32[2,512]{1,0:T(2,128)}, u32[]{:S(2)}) copy-start(f32[2,512]{1,0:T(2,128)} %get-tuple-element.85) | copy-start | bytes 12292
  342.7 13.3 %copy-start.12 = (f32[3,512]{1,0:T(4,128)S(1)}, f32[3,512]{1,0:T(4,128)}, u32[]{:S(2)}) copy-start(f32[3,512]{1,0:T(4,128)} %get-tuple-element.84) | copy-start | bytes 18436
  342.7 13.3 %copy-start.14 = (f32[2,512]{1,0:T(2,128)S(1)}, f32[2,512]{1,0:T(2,128)}, u32[]{:S(2)}) copy-start(f32[2,512]{1,0:T(2,128)} %get-tuple-element.83) | copy-start | bytes 12292
  350.8 38.2 %collective-permute-start.2 = (bf16[2,576,512]{2,1,0:T(8,128)(2,1)}, bf16[2,576,512]{2,1,0:T(8,128)(2,1)S(1)}, u32[]{:S(2)}, u32[]{:S(2)}) collective-permute-start(bf16[2,576,512]{2,1,0:T(8,128)(2,1)} %get-tuple-element.78), channel_id=1, source_target_pairs={{1,0},{2,1},{3,2},{4,3},{5,4},{6,5},{7,6},{8,7},{9,8},{10,9},{11,1... | collective-permute-start | bytes 3538952 | tf_op jit(solution)/shard_map/ppermute | solution.py:413
Sparse Core Ops, SparseCore 0:
  11.4 74.6 all-gather.4
  89.5 54.1 all-gather.2
  326.7 99.4 reduce-scatter.1
